TPU v7x, 512 devices: a whole 4x4x16 slice. The times are simulated.
512 devices in a mesh: dp: 16 (over y_lo, x, core), mp: 32 (over y_hi, z).
Axes of the slice: x: 4, y: 4 (y_hi: 2, y_lo: 2; y = y_hi * 2 + y_lo), z: 16, core: 2. Of those that a mesh axis runs over, the one named last changes fastest.
Arguments:
- tokens: bfloat16 [4096, 3072], P('dp', 'mp'), may hold values from -6 to 6
- gain: bfloat16 [3072], P('mp'), may hold values from 0.099609375 to 1.8984375
- w_qkv: bfloat16 [3072, 32, 384], P(None, 'mp'), may hold values from -0.21875 to 0.21875
- out_grad: bfloat16 [4096, 4096], P('dp', 'mp'), may hold values from -12 to 12
Outputs:
- attn_out: bfloat16 [4096, 4096], P('dp', 'mp')
- input_grad: bfloat16 [4096, 3072], P('dp', 'mp')
- weight_grad: float32 [3072, 32, 384], P('dp', 'mp')
- gain_grad: float32 [3072], P('mp')
All inputs are finite; a program needn't handle non-finite values.
Results may differ from a plain program's by a relative error of at most 0.03.
Values may be sent and summed in bfloat16 or wider, within the bound.
A program may use at most 64 MiB of HBM per device.

v0:
```python
import math

import jax
import jax.numpy as jnp
from jax import lax
from jax.sharding import PartitionSpec as P

D = 3072
PATCHES = 256


epsilon = 1e-06


def unit_rows(matrix):
    centred = matrix - jnp.mean(matrix, axis=-1, keepdims=True)
    return centred * lax.rsqrt(jnp.mean(centred * centred, axis=-1, keepdims=True) + epsilon)


def exact_attention(projected):
    head_width = projected.shape[1] // 3
    image_count = projected.shape[0] // PATCHES
    query = unit_rows(projected[:, :head_width]).reshape(image_count, PATCHES, head_width)
    key_rows = unit_rows(projected[:, head_width : 2 * head_width]).reshape(
        image_count, PATCHES, head_width
    )
    value_rows = projected[:, 2 * head_width :].reshape(image_count, PATCHES, head_width)
    scores = jnp.einsum("nqd,nkd->nqk", query, key_rows) / math.sqrt(head_width)
    exponent = jnp.exp(scores)
    weights_soft = exponent / jnp.sum(exponent, axis=-1, keepdims=True)
    return jnp.einsum("nqk,nkd->nqd", weights_soft, value_rows).reshape(-1, head_width)


def rounded_attention(projected):
    head_width = projected.shape[1] // 3
    image_count = projected.shape[0] // PATCHES
    widened = projected.astype(jnp.float32)
    query = (
        unit_rows(widened[:, :head_width])
        .astype(jnp.bfloat16)
        .reshape(image_count, PATCHES, head_width)
    )
    key_rows = (
        unit_rows(widened[:, head_width : 2 * head_width])
        .astype(jnp.bfloat16)
        .reshape(image_count, PATCHES, head_width)
    )
    value_rows = projected[:, 2 * head_width :].reshape(image_count, PATCHES, head_width)
    scores = jnp.einsum(
        "nqd,nkd->nqk", query, key_rows, preferred_element_type=jnp.float32
    ) / math.sqrt(head_width)
    exponent = jnp.exp(scores)
    weights_soft = (exponent / jnp.sum(exponent, axis=-1, keepdims=True)).astype(jnp.bfloat16)
    result = jnp.einsum(
        "nqk,nkd->nqd", weights_soft, value_rows, preferred_element_type=jnp.float32
    )
    return result.reshape(-1, head_width).astype(jnp.bfloat16)


def on_device(tokens, gain, w_qkv, out_grad):
    weights = w_qkv[:, 0, :]
    widened = tokens.astype(jnp.float32)
    totals, squares = lax.psum((jnp.sum(widened, axis=1), jnp.sum(widened * widened, axis=1)), "mp")
    average = totals / D
    inverse = lax.rsqrt(squares / D - average * average + epsilon)
    normed = (widened - average[:, None]) * inverse[:, None]
    normed_part = (normed * gain.astype(jnp.float32)).astype(jnp.bfloat16)
    normed_in = lax.all_gather(normed_part, "mp", axis=1, tiled=True)
    projected = jnp.dot(normed_in, weights, preferred_element_type=jnp.float32).astype(jnp.bfloat16)
    attended = rounded_attention(projected)
    _, pullback = jax.vjp(exact_attention, projected.astype(jnp.float32))
    head_grad = pullback(out_grad.astype(jnp.float32))[0].astype(jnp.bfloat16)
    weight_share = lax.psum_scatter(
        lax.dot_general(
            normed_in, head_grad, (((0,), (0,)), ((), ())), preferred_element_type=jnp.float32
        ).astype(jnp.bfloat16),
        "dp",
        scatter_dimension=0,
        tiled=True,
    ).astype(jnp.float32)
    input_pull = (
        lax.psum_scatter(
            lax.dot_general(
                weights, head_grad, (((1,), (1,)), ((), ())), preferred_element_type=jnp.float32
            ).astype(jnp.bfloat16),
            "mp",
            scatter_dimension=0,
            tiled=True,
        )
        .astype(jnp.float32)
        .T
    )
    scaled = input_pull * gain.astype(jnp.float32)
    plain_sum, cross_sum = lax.psum(
        (jnp.sum(scaled, axis=1), jnp.sum(scaled * normed, axis=1)), "mp"
    )
    input_grad = inverse[:, None] * (
        scaled - plain_sum[:, None] / D - normed * cross_sum[:, None] / D
    )
    gain_grad = lax.psum(jnp.sum(input_pull * normed, axis=0), "dp")
    return (attended, input_grad.astype(jnp.bfloat16), weight_share[:, None, :], gain_grad)


def solution(mesh):
    in_specs = (P("dp", "mp"), P("mp"), P(None, "mp", None), P("dp", "mp"))
    out_specs = (P("dp", "mp"), P("dp", "mp"), P("dp", "mp", None), P("mp"))
    return jax.shard_map(
        on_device, mesh=mesh, in_specs=in_specs, out_specs=out_specs, check_vma=False
    )
```

profile of v0, /device:TPU:1, one launch (start us, length us, event | category | flops | bytes accessed | tf_op | source)
XLA Modules:
  0.0 1000.1 jit_solution(11403737845114648216)
XLA Ops:
  7.2 0.0 copy-start
  7.2 0.0 all-gather.2.cloned.1.call-start
  7.2 0.8 convert_element_type.49
  8.0 0.8 convert_reduce_fusion
  8.9 70.7 %all-reduce.4 = (f32[256]{0:T(256)S(1)}, f32[256]{0:T(256)S(1)}) all-reduce(f32[256]{0:T(256)S(1)} %get-tuple-element.22, f32[256]{0:T(256)S(1)} %get-tuple-element.21), channel_id=1, replica_groups=mesh['dp'=16,'mp'=32] {'mp'}, use_global_device_ids=true, to_apply=%region_3.0 | all-reduce | flops 512 | bytes 4096 | tf_op jit(solution)/shard_map/psum | solution.py:63
  79.6 1.5 fusion.25
  81.1 0.0 all-gather.2.cloned.1.call-update
  81.1 0.0 copy-start.2
  81.1 0.0 reduce-scatter.7.cloned.1.call-start
  81.2 140.8 %all-gather.2.cloned.1.call-done = bf16[256,3072]{0,1:T(8,128)(2,1)} async-done(((bf16[256,96]{0,1:T(8,128)(2,1)}), bf16[256,3072]{0,1:T(8,128)(2,1)}) %all-gather.2.cloned.1.call-update) | async-done | bytes 1572880 | tf_op jit(solution)/shard_map/all_gather | solution.py:68
  222.0 0.0 copy-done
  222.0 2.4 fusion.50
  224.4 0.1 slice_reduce_fusion.1
  224.6 0.2 multiply_reduce_fusion.3
  224.9 0.3 fusion.52
  225.2 0.0 copy-done.2
  225.2 0.2 fusion.11
  225.4 0.2 fusion.10
  225.7 0.4 multiply_reduce_fusion.1
  226.0 0.5 fusion.46
  226.5 0.4 broadcast_add_fusion.1
  226.9 0.2 broadcast_add_fusion
  227.2 2.2 fusion
  229.3 2.6 copy.23
  231.9 0.0 reduce-scatter.7.cloned.1.call-update
  231.9 0.0 reduce-scatter.5.cloned.1.call-start
  232.0 3.8 convolution_convert_fusion
  235.8 0.0 copy-start.1
  235.8 0.0 reduce-scatter.5.cloned.1.call-update
  235.8 0.3 fusion.51
  236.2 0.9 convolution_convert_fusion.2
  237.0 652.6 %reduce-scatter.7.cloned.1.call-done = bf16[96,256]{1,0:T(8,128)(2,1)} async-done(((bf16[3072,256]{1,0:T(8,128)(2,1)}), bf16[96,256]{1,0:T(8,128)(2,1)}) %reduce-scatter.7.cloned.1.call-update) | async-done | bytes 49168 | tf_op jit(solution)/shard_map/reduce_scatter | solution.py:82
  889.7 0.0 copy-done.1
  889.7 1.0 fusion.31
  890.7 39.0 %psum.39 = f32[96]{0:T(128)} all-reduce(f32[96]{0:T(128)S(1)} %get-tuple-element.18), channel_id=1, replica_groups=mesh['dp'=16,'mp'=32] {'dp'}, use_global_device_ids=true, to_apply=%region_22.0 | all-reduce | flops 96 | bytes 768 | tf_op jit(solution)/shard_map/psum | solution.py:100
  929.6 60.5 %all-reduce.3 = (f32[256]{0:T(256)S(1)}, f32[256]{0:T(256)S(1)}) all-reduce(f32[256]{0:T(256)S(1)} %get-tuple-element.19, f32[256]{0:T(256)S(1)} %get-tuple-element.20), channel_id=1, replica_groups=mesh['dp'=16,'mp'=32] {'mp'}, use_global_device_ids=true, to_apply=%region_19.0 | all-reduce | flops 512 | bytes 4096 | tf_op jit(solution)/shard_map/psum | solution.py:94
  990.1 1.5 fusion.30
  991.6 0.0 reduce-scatter.5.cloned.1.call-done
  991.6 0.9 bitcast_convert_fusion
  992.6 1.0 copy.20
  (11 shorter events, 0.1 us)
Async XLA Ops:
  7.2 214.8 %copy-start = (bf16[3072,1,384]{2,0,1:T(8,128)(2,1)S(1)}, bf16[3072,1,384]{2,0,1:T(8,128)(2,1)}, u32[]{:S(2)}) copy-start(bf16[3072,1,384]{2,0,1:T(8,128)(2,1)} %param.6) | copy-start | bytes 7077892
  7.2 214.8 %all-gather.2.cloned.1.call-start = ((), (), s32[]{:S(2)}) async-start(), calls=%async_computation.2 | async-start | bytes 1622016 | tf_op jit(solution)/shard_map/all_gather | solution.py:68
  81.1 144.1 %copy-start.2 = (bf16[256,128]{1,0:T(8,128)(2,1)S(1)}, bf16[256,128]{1,0:T(8,128)(2,1)}, u32[]{:S(2)}) copy-start(bf16[256,128]{1,0:T(8,128)(2,1)} %param.7) | copy-start | bytes 196612
  81.1 808.5 %reduce-scatter.7.cloned.1.call-start = ((), (), s32[]{:S(2)}) async-start(), calls=%async_computation.4 | async-start | bytes 1622016 | tf_op jit(solution)/shard_map/reduce_scatter | solution.py:82
  231.9 759.7 %reduce-scatter.5.cloned.1.call-start = ((), (), s32[]{:S(2)}) async-start(), calls=%async_computation.3 | async-start | bytes 2506752 | tf_op jit(solution)/shard_map/reduce_scatter | solution.py:73
  235.8 653.9 %copy-start.1 = (bf16[256,96]{0,1:T(8,128)(2,1)S(1)}, bf16[256,96]{0,1:T(8,128)(2,1)}, u32[]{:S(2)}) copy-start(bf16[256,96]{0,1:T(8,128)(2,1)} %param.4) | copy-start | bytes 147460
Sparse Core Ops, SparseCore 0:
  81.3 140.6 all-gather.1
  232.1 657.5 reduce-scatter.6
  892.5 77.4 reduce-scatter.4
where the time goes:
time: 1010 us; the launch traced here: 1000 us
  waiting for transfers between devices  793 us (79%)
  blocking collectives  170 us (17%)
  between operations  13.9 us (1%)
  matrix products  11.2 us (1%)
    reduce_scatter x1, waiting for transfers between devices, on_device(): lax.psum_scatter(lax.dot_general(weights, head_grad, (((1,), (1,)), ((),...  653 us
    all_gather x1, waiting for transfers between devices, on_device(): normed_in = lax.all_gather(normed_part, 'mp', axis=1, tiled=True)  141 us
    psum x1, blocking collectives, on_device(): lax.psum((jnp.sum(widened, axis=1), jnp.sum(widened * widened, axis=1)),...  70.7 us
    psum x1, blocking collectives, on_device(): lax.psum((jnp.sum(scaled, axis=1), jnp.sum(scaled * normed, axis=1)), 'mp')  60.5 us
    psum x1, blocking collectives, on_device(): gain_grad = lax.psum(jnp.sum(input_pull * normed, axis=0), 'dp')  39 us
  transfers between devices with their start and end apart: 3, of which 2 were waited for; matrix products, arithmetic and copies ran while one was open for 1% of the time, Pallas kernels for 0%

commit v1 on v0

v1 whole, which is shorter than its diff:
```python
import math

import jax
import jax.numpy as jnp
from jax import lax
from jax.experimental import pallas as pl
from jax.experimental.pallas import tpu as pltpu
from jax.sharding import PartitionSpec as P

D = 3072
PATCHES = 256
HDIM = 128
FEAT = 96
NZ = 16
NY = 2
NMP = NZ * NY
CHIPS = 8
ROWS = 192
EPS = 1e-06
F32 = jnp.float32
BF16 = jnp.bfloat16
MESH = pl.DeviceIdType.MESH
VMEM = pltpu.VMEM


def ring_places():
    mp = lax.axis_index("mp")
    row, z = mp // NZ, mp % NZ
    right = row * NZ + (z + 1) % NZ
    left = row * NZ + (z + NZ - 1) % NZ
    partner = (1 - row) * NZ + z
    return mp, row, z, right, left, partner


def remote(src, dst, send_sem, recv_sem, target):
    return pltpu.make_async_remote_copy(
        src_ref=src,
        dst_ref=dst,
        send_sem=send_sem,
        recv_sem=recv_sem,
        device_id=target,
        device_id_type=MESH,
    )


def hops_of(direction, stream):
    return NZ // 2 if direction == stream else NZ // 2 - 1


def gather_kernel(x_ref, gain_ref, g_ref, gg_ref, send, recv, gsend, grecv, ysend, yrecv):
    mp, row, z, right, left, partner = ring_places()
    barrier = pltpu.get_barrier_semaphore()
    for peer in (right, left, partner):
        pl.semaphore_signal(barrier, inc=1, device_id={"mp": peer}, device_id_type=MESH)
    g_ref[mp] = x_ref[...]
    gg_ref[z, row] = jnp.concatenate(
        [gain_ref[...].astype(F32), jnp.zeros((1, 128 - FEAT), F32)], axis=1
    )
    pl.semaphore_wait(barrier, 3)

    ring = (right, left)
    ends = (row, 1 - row)

    def block_copy(direction, stream, hop, distance):
        source = (z - distance + NZ) % NZ if direction == 0 else (z + distance) % NZ
        ref = g_ref.at[ends[stream] * NZ + source]
        return remote(
            ref,
            ref,
            send.at[direction, stream, hop],
            recv.at[direction, stream, hop],
            {"mp": ring[direction]},
        )

    def gain_copy(direction, hop, distance):
        source = (z - distance + NZ) % NZ if direction == 0 else (z + distance) % NZ
        ref = gg_ref.at[source]
        return remote(
            ref, ref, gsend.at[direction, hop], grecv.at[direction, hop], {"mp": ring[direction]}
        )

    own, other = g_ref.at[mp], g_ref.at[partner]
    across = remote(own, own, ysend.at[0], yrecv.at[0], {"mp": partner})
    across.start()
    gown = gg_ref.at[z, row]
    gacross = remote(gown, gown, ysend.at[1], yrecv.at[1], {"mp": partner})
    gacross.start()
    for direction in (0, 1):
        block_copy(direction, 0, 0, 0).start()
    remote(other, other, ysend.at[0], yrecv.at[0], {"mp": partner}).wait_recv()
    for direction in (0, 1):
        block_copy(direction, 1, 0, 0).start()
    gother = gg_ref.at[z, 1 - row]
    remote(gother, gother, ysend.at[1], yrecv.at[1], {"mp": partner}).wait_recv()
    for direction in (0, 1):
        gain_copy(direction, 0, 0).start()
    for hop in range(1, NZ // 2 + 1):
        for stream in (0, 1):
            for direction in (0, 1):
                hops = hops_of(direction, stream)
                if hop <= hops:
                    block_copy(direction, stream, hop - 1, hop).wait_recv()
                if hop < hops:
                    block_copy(direction, stream, hop, hop).start()
        for direction in (0, 1):
            hops = hops_of(direction, 0)
            if hop <= hops:
                gain_copy(direction, hop - 1, hop).wait_recv()
            if hop < hops:
                gain_copy(direction, hop, hop).start()
    across.wait_send()
    gacross.wait_send()
    for direction in (0, 1):
        for stream in (0, 1):
            for hop in range(hops_of(direction, stream)):
                block_copy(direction, stream, hop, hop).wait_send()
        for hop in range(hops_of(direction, 0)):
            gain_copy(direction, hop, hop).wait_send()


def gather(x, gain):
    return pl.pallas_call(
        gather_kernel,
        out_shape=(
            jax.ShapeDtypeStruct((NMP, FEAT, PATCHES), BF16),
            jax.ShapeDtypeStruct((NZ, NY, 1, 128), F32),
        ),
        in_specs=[pl.BlockSpec(memory_space=VMEM)] * 2,
        out_specs=(pl.BlockSpec(memory_space=VMEM), pl.BlockSpec(memory_space=VMEM)),
        scratch_shapes=[
            pltpu.SemaphoreType.DMA((2, 2, 8)),
            pltpu.SemaphoreType.DMA((2, 2, 8)),
            pltpu.SemaphoreType.DMA((2, 8)),
            pltpu.SemaphoreType.DMA((2, 8)),
            pltpu.SemaphoreType.DMA((2,)),
            pltpu.SemaphoreType.DMA((2,)),
        ],
        compiler_params=pltpu.CompilerParams(
            collective_id=0, has_side_effects=True, vmem_limit_bytes=16 << 20
        ),
    )(x, gain)


def folded(matrix):
    return jnp.sum(matrix.reshape(matrix.shape[0] // 8, 8, matrix.shape[1]), axis=0)


def column_mean(matrix):
    return jnp.sum(matrix, axis=0, keepdims=True) * (1.0 / matrix.shape[0])


def unit_columns(matrix):
    centred = matrix - column_mean(matrix)
    inverse = lax.rsqrt(column_mean(centred * centred) + EPS)
    return centred * inverse, inverse


def unit_pullback(normal, inverse, cotangent):
    return inverse * (
        cotangent - column_mean(cotangent) - normal * column_mean(cotangent * normal)
    )


def dot(a, b):
    return jnp.dot(a, b, preferred_element_type=F32)


def dot_rows(a, b):
    return lax.dot_general(a, b, (((1,), (1,)), ((), ())), preferred_element_type=F32)


def compute_kernel(
    g_ref,
    gg_ref,
    w_ref,
    do_ref,
    att_ref,
    pull_ref,
    ws_ref,
    sums_ref,
    stats_ref,
    gown_ref,
    nt_ref,
    wt_ref,
    rows_ref,
    gb_ref,
    hg_ref,
):
    mp = lax.axis_index("mp")
    for part in range(D // 256):
        wt_ref[:, part * 256 : (part + 1) * 256] = w_ref[part * 256 : (part + 1) * 256, :].T
    for block in range(NMP):
        rows_ref[block : block + 1, :] = gg_ref[block % NZ, block // NZ]
    turned = rows_ref[...].T
    for block in range(NMP):
        gb_ref[block] = jnp.broadcast_to(turned[:FEAT, block : block + 1], (FEAT, 128)).astype(BF16)
    gown_ref[...] = gb_ref[mp].astype(F32)
    gain_weights = dot(wt_ref[...], gb_ref[...].reshape(D, 128))

    def add_sum(block, total):
        return total + folded(g_ref[block].astype(F32))

    total = lax.fori_loop(0, NMP, add_sum, jnp.zeros((8, PATCHES), F32))
    average = jnp.sum(total, axis=0, keepdims=True) * (1.0 / D)

    def add_square(block, total):
        centred = g_ref[block].astype(F32) - average
        return total + folded(centred * centred)

    total = lax.fori_loop(0, NMP, add_square, jnp.zeros((8, PATCHES), F32))
    inverse = lax.rsqrt(jnp.sum(total, axis=0, keepdims=True) * (1.0 / D) + EPS)
    stats_ref[0] = average
    stats_ref[1] = inverse

    def normalize(block, carry):
        factor = gb_ref[block].astype(F32)
        factor = jnp.concatenate([factor, factor], axis=1)
        normed = (g_ref[block].astype(F32) - average) * inverse
        nt_ref[block] = (normed * factor).astype(BF16)
        return carry

    lax.fori_loop(0, NMP, normalize, 0)

    wide = dot(wt_ref[...], nt_ref[...].reshape(D, PATCHES))
    projected = wide.astype(BF16)
    query, query_inverse = unit_columns(projected[:HDIM].astype(F32))
    keys, keys_inverse = unit_columns(projected[HDIM : 2 * HDIM].astype(F32))
    values = projected[2 * HDIM :]
    query_r, keys_r = query.astype(BF16), keys.astype(BF16)
    scale = 1.0 / math.sqrt(HDIM)
    exponent = jnp.exp(dot(keys_r.T, query_r) * scale)
    soft = exponent / jnp.sum(exponent, axis=0, keepdims=True)
    soft_r = soft.astype(BF16)
    att_ref[...] = dot(values, soft_r).T.astype(BF16)
    cotangent = do_ref[...].T
    soft_grad = dot(values.T, cotangent)
    values_grad = dot_rows(cotangent, soft_r)
    score_grad = soft * (soft_grad - jnp.sum(soft * soft_grad, axis=0, keepdims=True))
    score_grad = (score_grad * scale).astype(BF16)
    query_grad = unit_pullback(query, query_inverse, dot(keys_r, score_grad))
    keys_grad = unit_pullback(keys, keys_inverse, dot_rows(query_r, score_grad))
    hg = jnp.concatenate([query_grad, keys_grad, values_grad], axis=0).astype(BF16)
    hg_ref[...] = hg
    hg_wide = hg.astype(F32)
    factor = jnp.concatenate([gain_weights, gain_weights], axis=1)
    sums_ref[0] = jnp.sum(hg_wide * factor, axis=0, keepdims=True)
    sums_ref[1] = jnp.sum(hg_wide * wide, axis=0, keepdims=True)

    def pull_part(part, carry):
        block = dot(w_ref[pl.ds(pl.multiple_of(part * 384, 384), 384), :], hg_ref[...])
        pull_ref[pl.ds(part * 4, 4)] = block.astype(BF16).reshape(4, FEAT, PATCHES)
        return carry

    lax.fori_loop(0, 8, pull_part, 0)

    def weight_part(part, carry):
        block = dot_rows(nt_ref[pl.ds(part * 4, 4)].reshape(384, PATCHES), hg_ref[...])
        ws_ref[pl.ds(part * 2, 2)] = block.astype(BF16).reshape(2, ROWS, 3 * HDIM)
        return carry

    lax.fori_loop(0, 8, weight_part, 0)


def compute(g, gg, weights, out_grad):
    return pl.pallas_call(
        compute_kernel,
        out_shape=(
            jax.ShapeDtypeStruct((PATCHES, HDIM), BF16),
            jax.ShapeDtypeStruct((NMP, FEAT, PATCHES), BF16),
            jax.ShapeDtypeStruct((2 * CHIPS, ROWS, 3 * HDIM), BF16),
            jax.ShapeDtypeStruct((2, 1, PATCHES), F32),
            jax.ShapeDtypeStruct((2, 1, PATCHES), F32),
            jax.ShapeDtypeStruct((FEAT, 128), F32),
        ),
        in_specs=[pl.BlockSpec(memory_space=VMEM)] * 4,
        out_specs=tuple([pl.BlockSpec(memory_space=VMEM)] * 6),
        scratch_shapes=[
            VMEM((NMP, FEAT, PATCHES), BF16),
            VMEM((3 * HDIM, D), BF16),
            VMEM((NMP, 128), F32),
            VMEM((NMP, FEAT, 128), BF16),
            VMEM((3 * HDIM, PATCHES), BF16),
        ],
        compiler_params=pltpu.CompilerParams(vmem_limit_bytes=40 << 20),
    )(g, gg, weights, out_grad)


def scatter_kernel(
    pull_ref,
    ws_ref,
    sums_ref,
    stats_ref,
    gown_ref,
    x_ref,
    ig_ref,
    wg_ref,
    gg_ref,
    land,
    ystage,
    yland,
    tot,
    spair,
    sland,
    cland,
    dland,
    gland,
    gstage,
    send,
    recv,
    ssend,
    srecv,
    ysend,
    yrecv,
    csend,
    crecv,
    dsend,
    drecv,
    gsend,
    grecv,
):
    mp, row, z, right, left, partner = ring_places()
    dp = lax.axis_index("dp")
    chip, core = dp // 2, dp % 2
    barrier = pltpu.get_barrier_semaphore()
    for peer in (right, left, partner):
        pl.semaphore_signal(barrier, inc=1, device_id={"mp": peer}, device_id_type=MESH)
    mate = chip * 2 + 1 - core
    pl.semaphore_signal(barrier, inc=1, device_id={"dp": mate}, device_id_type=MESH)

    def chip_at(shift):
        line, place = chip // 4, chip % 4
        return ((line + shift // 4) % 2) * 4 + (place + shift % 4) % 4

    for shift in range(1, CHIPS):
        pl.semaphore_signal(
            barrier, inc=1, device_id={"dp": chip_at(shift) * 2 + core}, device_id_type=MESH
        )
    pl.semaphore_wait(barrier, 3 + 1 + CHIPS - 1)

    ring = (right, left)
    ends = (row, 1 - row)

    def target(direction, stream, left_over):
        place = (z + left_over) % NZ if direction == 0 else (z - left_over + NZ) % NZ
        return ends[stream] * NZ + place

    def ring_copy(direction, stream, hop):
        hops = hops_of(direction, stream)
        if hop == 0:
            src = pull_ref.at[target(direction, stream, hops)]
        else:
            src = land.at[direction, stream, hop - 1]
        return remote(
            src,
            land.at[direction, stream, hop],
            send.at[direction, stream, hop],
            recv.at[direction, stream, hop],
            {"mp": ring[direction]},
        )

    def sum_copy(direction, hop, distance):
        source = (z - distance + NZ) % NZ if direction == 0 else (z + distance) % NZ
        ref = sland.at[source]
        return remote(
            ref, ref, ssend.at[direction, hop], srecv.at[direction, hop], {"mp": ring[direction]}
        )

    def core_copy(shift):
        to = chip_at(shift)
        return remote(
            ws_ref.at[to * 2 + 1 - core],
            cland.at[to],
            csend.at[shift],
            crecv.at[shift],
            {"dp": mate},
        )

    def chip_copy(shift):
        to = chip_at(shift)
        return remote(
            cland.at[to],
            dland.at[shift],
            dsend.at[shift],
            drecv.at[shift],
            {"dp": to * 2 + core},
        )

    def chip_step(shift):
        core_copy(shift).wait_recv()
        to = chip_at(shift)
        both = cland[to].astype(F32) + ws_ref[to * 2 + core].astype(F32)
        if shift == 0:
            wg_ref[...] = both
        else:
            cland[to] = both.astype(BF16)
            chip_copy(shift).start()

    sums_across = remote(sums_ref, spair, ysend.at[1], yrecv.at[1], {"mp": partner})
    sums_across.start()
    for stream in (1, 0):
        for direction in (0, 1):
            ring_copy(direction, stream, 0).start()
    order = (6, 2, 5, 7, 4, 1, 3, 0)
    for shift in order:
        core_copy(shift).start()
    sums_across.wait_recv()
    sland[z] = sums_ref[...] + spair[...]
    for direction in (0, 1):
        sum_copy(direction, 0, 0).start()
    for hop in range(1, NZ // 2 + 1):
        for stream in (1, 0):
            for direction in (0, 1):
                hops = hops_of(direction, stream)
                if hop <= hops:
                    ring_copy(direction, stream, hop - 1).wait_recv()
                if hop < hops:
                    slot = land.at[direction, stream, hop - 1]
                    mine = pull_ref[target(direction, stream, hops - hop)]
                    slot[...] = (slot[...].astype(F32) + mine.astype(F32)).astype(BF16)
                    ring_copy(direction, stream, hop).start()
        for direction in (0, 1):
            hops = hops_of(direction, 0)
            if hop <= hops:
                sum_copy(direction, hop - 1, hop).wait_recv()
            if hop < hops:
                sum_copy(direction, hop, hop).start()
        if hop < NZ // 2:
            chip_step(order[hop - 1])
    half = NZ // 2
    ystage[...] = (
        pull_ref[partner].astype(F32)
        + land[0, 1, half - 2].astype(F32)
        + land[1, 1, half - 1].astype(F32)
    ).astype(BF16)
    across = remote(ystage, yland, ysend.at[0], yrecv.at[0], {"mp": partner})
    across.start()
    chip_step(order[half - 1])
    tot[...] = (
        pull_ref[mp].astype(F32)
        + land[0, 0, half - 1].astype(F32)
        + land[1, 0, half - 2].astype(F32)
    )
    sums = sland[0]
    for place in range(1, NZ):
        sums = sums + sland[place]
    average, inverse = stats_ref[0], stats_ref[1]
    normed = (x_ref[...].astype(F32) - average) * inverse
    across.wait_recv()
    pull = tot[...] + yland[...].astype(F32)
    cross = pull * normed
    turned = (cross[:, :128] + cross[:, 128:]).T
    gstage[0] = jnp.concatenate(
        [jnp.sum(turned, axis=0, keepdims=True), jnp.zeros((1, 128 - FEAT), F32)], axis=1
    )
    gain_core = remote(gstage.at[0], gland.at[0], gsend.at[0], grecv.at[0], {"dp": mate})
    gain_core.start()
    gain_own = gown_ref[...]
    scaled = pull * jnp.concatenate([gain_own, gain_own], axis=1)
    ig_ref[...] = (
        inverse * (scaled - sums[0] * (1.0 / D) - normed * (sums[1] * (1.0 / D)))
    ).astype(BF16)
    gain_core.wait_recv()
    gstage[1] = gstage[0] + gland[0]

    def gain_copy(shift):
        return remote(
            gstage.at[1],
            gland.at[shift],
            gsend.at[shift],
            grecv.at[shift],
            {"dp": chip_at(shift) * 2 + core},
        )

    for shift in range(1, CHIPS):
        gain_copy(shift).start()
    for shift in order[:-1]:
        chip_copy(shift).wait_recv()
        wg_ref[...] += dland[shift].astype(F32)
    gain_total = gstage[1]
    for shift in range(1, CHIPS):
        gain_copy(shift).wait_recv()
        gain_total = gain_total + gland[shift]
    gg_ref[...] = gain_total
    sums_across.wait_send()
    across.wait_send()
    gain_core.wait_send()
    for direction in (0, 1):
        for stream in (0, 1):
            for hop in range(hops_of(direction, stream)):
                ring_copy(direction, stream, hop).wait_send()
        for hop in range(hops_of(direction, 0)):
            sum_copy(direction, hop, hop).wait_send()
    for shift in range(CHIPS):
        core_copy(shift).wait_send()
        if shift > 0:
            chip_copy(shift).wait_send()
            gain_copy(shift).wait_send()


def scatter(pull, share, sums, stats, gain_own, x):
    dma = pltpu.SemaphoreType.DMA
    return pl.pallas_call(
        scatter_kernel,
        out_shape=(
            jax.ShapeDtypeStruct((FEAT, PATCHES), BF16),
            jax.ShapeDtypeStruct((ROWS, 3 * HDIM), F32),
            jax.ShapeDtypeStruct((1, 128), F32),
        ),
        in_specs=[pl.BlockSpec(memory_space=VMEM)] * 6,
        out_specs=tuple([pl.BlockSpec(memory_space=VMEM)] * 3),
        scratch_shapes=[
            VMEM((2, 2, 8, FEAT, PATCHES), BF16),
            VMEM((FEAT, PATCHES), BF16),
            VMEM((FEAT, PATCHES), BF16),
            VMEM((FEAT, PATCHES), F32),
            VMEM((2, 1, PATCHES), F32),
            VMEM((NZ, 2, 1, PATCHES), F32),
            VMEM((CHIPS, ROWS, 3 * HDIM), BF16),
            VMEM((CHIPS, ROWS, 3 * HDIM), BF16),
            VMEM((CHIPS, 1, 128), F32),
            VMEM((2, 1, 128), F32),
            dma((2, 2, 8)),
            dma((2, 2, 8)),
            dma((2, 8)),
            dma((2, 8)),
            dma((2,)),
            dma((2,)),
            dma((CHIPS,)),
            dma((CHIPS,)),
            dma((CHIPS,)),
            dma((CHIPS,)),
            dma((CHIPS,)),
            dma((CHIPS,)),
        ],
        compiler_params=pltpu.CompilerParams(
            collective_id=1, has_side_effects=True, vmem_limit_bytes=40 << 20
        ),
    )(pull, share, sums, stats, gain_own, x)


def on_device(tokens, gain, w_qkv, out_grad):
    x = tokens.T
    gathered, gains = gather(x, gain.reshape(1, FEAT))
    attended, pull, share, sums, stats, gain_own = compute(
        gathered, gains, w_qkv[:, 0, :], out_grad
    )
    input_grad, weight_grad, gain_grad = scatter(pull, share, sums, stats, gain_own, x)
    return attended, input_grad.T, weight_grad[:, None, :], gain_grad[0, :FEAT]


def solution(mesh):
    in_specs = (P("dp", "mp"), P("mp"), P(None, "mp", None), P("dp", "mp"))
    out_specs = (P("dp", "mp"), P("dp", "mp"), P("dp", "mp", None), P("mp"))
    return jax.shard_map(
        on_device, mesh=mesh, in_specs=in_specs, out_specs=out_specs, check_vma=False
    )
```

time: 1010 us -> 107 us (0.11)
  waiting for transfers between devices: 793 us -> 0 us
  blocking collectives: 170 us -> 0 us
  Pallas kernels: 0 us -> 99.5 us
  between operations: 13.9 us -> 0.67 us
  matrix products: 11.2 us -> 0 us
    reduce_scatter x2 -> x0, waiting for transfers between devices: 653 us -> none  [the longest x1 653 us: on_device(): lax.psum_scatter(lax.dot_general(weights, head_grad, (((1,), (1,)), ((),...]
    psum x3 -> x0, blocking collectives: 170 us -> none  [the longest x1 70.7 us: on_device(): lax.psum((jnp.sum(widened, axis=1), jnp.sum(widened * widened, axis=1)),...]
    all_gather x1 -> x0, waiting for transfers between devices: 141 us -> none  [on_device(): normed_in = lax.all_gather(normed_part, 'mp', axis=1, tiled=True)]
    pallas_call x0 -> x3, Pallas kernels: none -> 99.5 us  [the longest x1 49.6 us: scatter(): pl.pallas_call(scatter_kernel, out_shape=(jax.ShapeDtypeStruct((FEAT, PAT...]
    dot_general x10 -> x0, matrix products: 11.2 us -> none  [the longest x1 3.8 us: on_device(): lax.dot_general(normed_in, head_grad, (((0,), (0,)), ((), ())), preferred...]
  transfers between devices with their start and end apart: 3 -> 0, of which waited for: 2 -> 0; matrix products, arithmetic and copies ran while one was open for 1% -> 0% of each run, Pallas kernels for 0% -> 0%
where the time goes in v1:
time: 107 us; the launch traced here: 106 us
  Pallas kernels  99.5 us (93%)
  local copies, waits for them, and re-layouts  6.1 us (6%)
    pallas_call x1, Pallas kernels, scatter(): pl.pallas_call(scatter_kernel, out_shape=(jax.ShapeDtypeStruct((FEAT, PAT...  49.6 us
    pallas_call x1, Pallas kernels, gather(): pl.pallas_call(gather_kernel, out_shape=(jax.ShapeDtypeStruct((NMP, FEAT,...  39.4 us
    pallas_call x1, Pallas kernels, compute(): pl.pallas_call(compute_kernel, out_shape=(jax.ShapeDtypeStruct((PATCHES,...  10.4 us
    unnamed x12, local copies, waits for them, and re-layouts  5.59 us

profile of v1, /device:TPU:1, one launch (start us, length us, event | category | flops | bytes accessed | tf_op | source)
XLA Modules:
  0.0 106.2 jit_solution(2529357106829034973)
XLA Ops:
  0.6 0.0 copy-start.1
  0.6 0.8 copy-done.1
  1.4 0.0 copy-start.4
  1.4 0.7 copy-done.4
  2.1 0.0 copy-start.2
  2.1 39.4 %shard_map.75 = (bf16[32,96,256]{2,1,0:T(8,128)(2,1)S(1)}, f32[16,2,1,128]{3,2,1,0:T(1,128)S(1)}) custom-call(bf16[96,256]{1,0:T(8,128)(2,1)S(1)} %bitcast.9, bf16[1,96]{1,0:T(2,128)(2,1)S(1)} %bitcast.12), custom_call_target="tpu_custom_call" | custom-call | tf_op jit(solution)/shard_map/pallas_call | solution.py:122
  41.5 0.0 copy-start
  41.5 1.7 %copy-done = bf16[3072,1,384]{2,0,1:T(8,128)(2,1)S(1)} copy-done((bf16[3072,1,384]{2,0,1:T(8,128)(2,1)S(1)}, bf16[3072,1,384]{2,0,1:T(8,128)(2,1)}, u32[]{:S(2)}) %copy-start) | copy-done | bytes 2359320
  43.2 0.0 copy-start.3
  43.2 0.8 copy-done.3
  44.0 10.4 %shard_map.76 = (bf16[256,128]{1,0:T(8,128)(2,1)}, bf16[32,96,256]{2,1,0:T(8,128)(2,1)S(1)}, bf16[16,192,384]{2,1,0:T(8,128)(2,1)S(1)}, f32[2,1,256]{2,1,0:T(1,1...) custom-call(bf16[32,96,256]{2,1,0:T(8,128)(2,1)S(1)} %get-tuple-element.15.g_ref, ...), custom_call_target="tpu_custom_call" | custom-call | tf_op jit(solution)/shard_map/pallas_call | solution.py:265
  54.4 0.0 copy-done.2
  54.4 49.6 %shard_map.77 = (bf16[96,256]{1,0:T(8,128)(2,1)S(1)}, f32[192,384]{1,0:T(8,128)S(1)}, f32[1,128]{1,0:T(1,128)S(1)}) custom-call(bf16[32,96,256]{2,1,0:T(8,128)(2,1)S(1)} %get-tuple-element.18.pull_ref, bf16[16,192,384]{2,1,0:T(8,128)(2,1)S(1)} %get-tuple-element.19.ws_ref, f32[2,1,256]{2,1,0:T(1,128)S(1)} %get-tuple-element.20.sums_ref, ...), custom_call_target="tpu_custom_call" | custom-call | tf_op jit(solution)/shard_map/pallas_call | solution.py:502
  104.1 1.0 copy.8
  105.1 0.5 slice_bitcast_fusion
  105.6 0.6 copy.10
Async XLA Ops:
  0.6 0.8 copy-start.1
  1.4 0.7 copy-start.4
  2.1 52.3 %copy-start.2 = (bf16[256,96]{0,1:T(8,128)(2,1)S(1)}, bf16[256,96]{0,1:T(8,128)(2,1)}, u32[]{:S(2)}) copy-start(bf16[256,96]{0,1:T(8,128)(2,1)} %param.4) | copy-start | bytes 147460
  41.5 1.7 %copy-start = (bf16[3072,1,384]{2,0,1:T(8,128)(2,1)S(1)}, bf16[3072,1,384]{2,0,1:T(8,128)(2,1)}, u32[]{:S(2)}) copy-start(bf16[3072,1,384]{2,0,1:T(8,128)(2,1)} %param.6) | copy-start | bytes 7077892
  43.2 0.8 copy-start.3

commit v2 on v0

v2 whole, which is shorter than its diff:
```python
import math

import jax
import jax.numpy as jnp
from jax import lax
from jax.experimental import pallas as pl
from jax.experimental.pallas import tpu as pltpu
from jax.sharding import PartitionSpec as P

D = 3072
PATCHES = 256
HDIM = 128
FEAT = 96
NZ = 16
NY = 2
NMP = NZ * NY
CHIPS = 8
ROWS = 192
EPS = 1e-06
F32 = jnp.float32
BF16 = jnp.bfloat16
MESH = pl.DeviceIdType.MESH
VMEM = pltpu.VMEM


def remote(src, dst, send_sem, recv_sem, target):
    return pltpu.make_async_remote_copy(
        src_ref=src,
        dst_ref=dst,
        send_sem=send_sem,
        recv_sem=recv_sem,
        device_id=target,
        device_id_type=MESH,
    )


def folded(matrix):
    return jnp.sum(matrix.reshape(matrix.shape[0] // 8, 8, matrix.shape[1]), axis=0)


def column_mean(matrix):
    return jnp.sum(matrix, axis=0, keepdims=True) * (1.0 / matrix.shape[0])


def unit_columns(matrix):
    centred = matrix - column_mean(matrix)
    inverse = lax.rsqrt(column_mean(centred * centred) + EPS)
    return centred * inverse, inverse


def unit_pullback(normal, inverse, cotangent):
    return inverse * (
        cotangent - column_mean(cotangent) - normal * column_mean(cotangent * normal)
    )


def dot(a, b):
    return jnp.dot(a, b, preferred_element_type=F32)


def dot_rows(a, b):
    return lax.dot_general(a, b, (((1,), (1,)), ((), ())), preferred_element_type=F32)


def hub_of(offset):
    sign = 1 if offset > 0 else -1
    return sign * {1: 0, 3: 0, 2: 3, 4: 3, 6: 3, 5: 6, 7: 6}[abs(offset)]


LEAVES = (5, -5, 7, -7, 8, 2, -2, 4, -4)


def fused_kernel(
    x_any,
    gain_ref,
    w_any,
    do_any,
    att_ref,
    ig_ref,
    wg_ref,
    gg_ref,
    w_ref,
    do_ref,
    g_ref,
    gains,
    wt_ref,
    rows_ref,
    gb_ref,
    nt_ref,
    hg_ref,
    pull_ref,
    ws_ref,
    zland,
    yland,
    oland,
    ostage,
    sums,
    spair,
    sland,
    cland,
    xland,
    hland,
    hstage,
    gstage,
    gland,
    local,
    zsend,
    zrecv,
    ysend,
    yrecv,
    osend,
    orecv,
    psend,
    precv,
    psend2,
    precv2,
    qsend,
    qrecv,
    rzsend,
    rzrecv,
    rysend,
    ryrecv,
    rosend,
    rorecv,
    csend,
    crecv,
    xsend,
    xrecv,
    hsend,
    hrecv,
    gsend,
    grecv,
):
    mp = lax.axis_index("mp")
    row, z = mp // NZ, mp % NZ
    dp = lax.axis_index("dp")
    line, place, core = dp // 8, (dp // 2) % 4, dp % 2
    sign8 = 1 - 2 * core
    mine, theirs = row * NZ, (1 - row) * NZ
    partner = {"mp": theirs + z}

    def along(offset):
        return (z + offset + 2 * NZ) % NZ

    def at_z(offset):
        return {"mp": mine + along(offset)}

    def at_dp(line_of, place_of, core_of):
        return {"dp": (line_of * 4 + place_of) * 2 + core_of}

    def place_at(shift):
        return (place + shift) % 4

    mate = at_dp(line, place, 1 - core)
    across_line = at_dp(1 - line, place, core)

    own_copy = pltpu.make_async_copy(x_any, g_ref.at[mp], local.at[0])
    w_copy = pltpu.make_async_copy(w_any, w_ref, local.at[1])
    do_copy = pltpu.make_async_copy(do_any, do_ref, local.at[2])
    own_copy.start()
    w_copy.start()
    do_copy.start()
    barrier = pltpu.get_barrier_semaphore()
    peers = [at_z(offset) for offset in range(1, NZ)] + [partner, mate, across_line]
    peers += [at_dp(line, place_at(shift), core) for shift in (1, 2, 3)]
    for peer in peers:
        pl.semaphore_signal(barrier, inc=1, device_id=peer, device_id_type=MESH)
    gains[z, row] = jnp.concatenate(
        [gain_ref[...].astype(F32), jnp.zeros((1, 128 - FEAT), F32)], axis=1
    )
    own_copy.wait()
    pl.semaphore_wait(barrier, len(peers))

    def spread(offset):
        hub = 6 * sign8 if offset == 8 else hub_of(offset)
        block = g_ref.at[mine + along(-hub)]
        step = offset - hub
        slot = offset % NZ
        return remote(block, block, zsend.at[slot], zrecv.at[slot], at_z(step))

    def arrived(offset):
        block = g_ref.at[mine + along(-offset)]
        slot = offset % NZ
        remote(block, block, zsend.at[slot], zrecv.at[slot], at_z(1)).wait_recv()

    def over(offset):
        block = g_ref.at[mine + along(-offset)]
        slot = offset % NZ
        return remote(block, block, ysend.at[slot], yrecv.at[slot], partner)

    def over_arrived(offset):
        block = g_ref.at[theirs + along(-offset)]
        slot = offset % NZ
        remote(block, block, ysend.at[slot], yrecv.at[slot], partner).wait_recv()

    def other(which, offset):
        block = g_ref.at[theirs + z]
        return remote(block, block, osend.at[which], orecv.at[which], at_z(offset))

    def other_arrived(which, offset):
        block = g_ref.at[theirs + along(-offset)]
        remote(block, block, osend.at[which], orecv.at[which], at_z(offset)).wait_recv()

    def gain_to(offset):
        pair = gains.at[z]
        return remote(pair, pair, psend.at[offset], precv.at[offset], at_z(offset))

    for offset in (3, -3):
        spread(offset).start()
    over(0).start()
    for offset in (1, -1):
        spread(offset).start()
    gown = gains.at[z, row]
    gain_over = remote(gown, gown, psend2.at[0], precv2.at[0], partner)
    gain_over.start()
    w_copy.wait()
    for part in range(D // 256):
        wt_ref[:, part * 256 : (part + 1) * 256] = w_ref[part * 256 : (part + 1) * 256, :].T
    over_arrived(0)
    for which, offset in enumerate((1, -1)):
        other(which, offset).start()
    for sign in (1, -1):
        arrived(3 * sign)
        for offset in (6 * sign, 4 * sign, 2 * sign):
            spread(offset).start()
        over(3 * sign).start()
    gother = gains.at[z, 1 - row]
    remote(gother, gother, psend2.at[0], precv2.at[0], partner).wait_recv()
    for offset in range(1, NZ):
        gain_to(offset).start()
    for sign in (1, -1):
        arrived(6 * sign)
        for offset in (5 * sign, 7 * sign):
            spread(offset).start()
        over(6 * sign).start()
    spread(8).start()
    arrived(1)
    arrived(-1)
    for offset in (2, -2, 4, -4, 5, -5, 7, -7, 8):
        arrived(offset)
        over(offset).start()
    for offset in range(1, NZ):
        pair = gains.at[along(-offset)]
        remote(pair, pair, psend.at[offset], precv.at[offset], at_z(offset)).wait_recv()
    for block in range(NMP):
        rows_ref[block : block + 1, :] = gains[block % NZ, block // NZ]
    turned = rows_ref[...].T
    for block in range(NMP):
        gb_ref[block] = jnp.broadcast_to(turned[:FEAT, block : block + 1], (FEAT, 128)).astype(BF16)
    gain_weights = dot(wt_ref[...], gb_ref[...].reshape(D, 128))
    do_copy.wait()
    cotangent = do_ref[...].T

    shift_row = jnp.sum(g_ref[mp].astype(F32), axis=0, keepdims=True) * (1.0 / FEAT)

    def add_block(block, totals):
        moved = g_ref[block].astype(F32) - shift_row
        return totals[0] + folded(moved), totals[1] + folded(moved * moved)

    zero = jnp.zeros((8, PATCHES), F32)
    totals = lax.fori_loop(mine, mine + NZ, add_block, (zero, zero))
    other_arrived(0, 1)
    other_arrived(1, -1)
    for offset in (3, -3, 6, -6, 2, -2, 4, -4, 5, -5, 7, -7, 8):
        over_arrived(offset)
    totals = lax.fori_loop(theirs, theirs + NZ, add_block, totals)
    first = jnp.sum(totals[0], axis=0, keepdims=True) * (1.0 / D)
    second = jnp.sum(totals[1], axis=0, keepdims=True) * (1.0 / D)
    average = shift_row + first
    inverse = lax.rsqrt(second - first * first + EPS)

    def normalize(block, carry):
        factor = gb_ref[block].astype(F32)
        factor = jnp.concatenate([factor, factor], axis=1)
        normed = (g_ref[block].astype(F32) - average) * inverse
        nt_ref[block] = (normed * factor).astype(BF16)
        return carry

    lax.fori_loop(0, NMP, normalize, 0)

    wide = dot(wt_ref[...], nt_ref[...].reshape(D, PATCHES))
    projected = wide.astype(BF16)
    query, query_inverse = unit_columns(projected[:HDIM].astype(F32))
    keys, keys_inverse = unit_columns(projected[HDIM : 2 * HDIM].astype(F32))
    values = projected[2 * HDIM :]
    query_r, keys_r = query.astype(BF16), keys.astype(BF16)
    scale = 1.0 / math.sqrt(HDIM)
    exponent = jnp.exp(dot(keys_r.T, query_r) * scale)
    soft = exponent / jnp.sum(exponent, axis=0, keepdims=True)
    soft_r = soft.astype(BF16)
    soft_grad = dot(values.T, cotangent)
    values_grad = dot_rows(cotangent, soft_r)
    score_grad = soft * (soft_grad - jnp.sum(soft * soft_grad, axis=0, keepdims=True))
    score_grad = (score_grad * scale).astype(BF16)
    query_grad = unit_pullback(query, query_inverse, dot(keys_r, score_grad))
    keys_grad = unit_pullback(keys, keys_inverse, dot_rows(query_r, score_grad))
    hg = jnp.concatenate([query_grad, keys_grad, values_grad], axis=0).astype(BF16)
    hg_ref[...] = hg

    def pull_rows(start):
        def pull_part(part, carry):
            block = start + part * 4
            rows = pl.ds(pl.multiple_of(block * FEAT, 4 * FEAT), 4 * FEAT)
            pull_ref[pl.ds(block, 4)] = (
                dot(w_ref[rows, :], hg_ref[...]).astype(BF16).reshape(4, FEAT, PATCHES)
            )
            return carry

        lax.fori_loop(0, 4, pull_part, 0)

    def back_over(offset):
        slot = offset % NZ
        src = ostage if offset == 0 else pull_ref.at[theirs + along(-offset)]
        return remote(src, yland.at[slot], rysend.at[slot], ryrecv.at[slot], partner)

    def back_other(which, offset):
        return remote(
            pull_ref.at[theirs + along(-offset)],
            oland.at[which],
            rosend.at[which],
            rorecv.at[which],
            at_z(-offset),
        )

    def back(offset):
        hub = 6 * sign8 if offset == 8 else hub_of(offset)
        slot = offset % NZ
        return remote(
            pull_ref.at[mine + along(-offset)],
            zland.at[slot],
            rzsend.at[slot],
            rzrecv.at[slot],
            at_z(hub - offset),
        )

    def gathered(offset, inputs):
        slot = offset % NZ
        back_over(offset).wait_recv()
        total = pull_ref[mine + along(-offset)].astype(F32) + yland[slot].astype(F32)
        for at in inputs:
            back(at).wait_recv()
            total = total + zland[at % NZ].astype(F32)
        return total

    def pass_on(offset, total):
        pull_ref[mine + along(-offset)] = total.astype(BF16)
        back(offset).start()

    pull_rows(theirs)
    for which, offset in enumerate((1, -1)):
        back_other(which, offset).start()
    for offset in (5, -5, 7, -7, 8, 6, -6, 2, -2, 4, -4, 3, -3):
        back_over(offset).start()

    def core_copy(shift, line_of):
        chip = line_of * 4 + place_at(shift)
        slot = shift * 2 + line_of
        return remote(
            ws_ref.at[chip * 2 + 1 - core],
            cland.at[shift, line_of],
            csend.at[slot],
            crecv.at[slot],
            mate,
        )

    def core_sum(shift, line_of):
        chip = line_of * 4 + place_at(shift)
        core_copy(shift, line_of).wait_recv()
        both = cland[shift, line_of].astype(F32) + ws_ref[chip * 2 + core].astype(F32)
        cland[shift, line_of] = both.astype(BF16)

    def place_copy(shift):
        return remote(
            cland.at[shift],
            xland.at[shift - 1],
            xsend.at[shift - 1],
            xrecv.at[shift - 1],
            at_dp(line, place_at(shift), core),
        )

    shifts = (2, 1, 3, 0)
    for shift in shifts:
        for line_of in (0, 1):
            chip = line_of * 4 + place_at(shift)
            block = dot_rows(nt_ref[pl.ds(chip * 4, 4)].reshape(4 * FEAT, PATCHES), hg_ref[...])
            ws_ref[pl.ds(chip * 2, 2)] = block.astype(BF16).reshape(2, ROWS, 3 * HDIM)
            core_copy(shift, line_of).start()
    hg_wide = hg.astype(F32)
    factor = jnp.concatenate([gain_weights, gain_weights], axis=1)
    sums[0] = jnp.sum(hg_wide * factor, axis=0, keepdims=True)
    sums[1] = jnp.sum(hg_wide * wide, axis=0, keepdims=True)
    sums_over = remote(sums, spair, psend2.at[1], precv2.at[1], partner)
    sums_over.start()
    pull_rows(mine)
    for offset in (1, -1):
        back(offset).start()
    att_ref[...] = dot(values, soft_r).T.astype(BF16)

    def leaf(offset):
        pass_on(offset, gathered(offset, ()))

    for offset in (5, -5, 7, -7):
        leaf(offset)
    for shift in shifts[:-1]:
        core_sum(shift, 0)
        core_sum(shift, 1)
        place_copy(shift).start()
    leaf(8)
    sums_over.wait_recv()
    sland[z] = sums[...] + spair[...]

    def sums_to(offset):
        pair = sland.at[z]
        return remote(pair, pair, qsend.at[offset], qrecv.at[offset], at_z(offset))

    for offset in range(1, NZ):
        sums_to(offset).start()
    for which, offset in enumerate((1, -1)):
        back_other(which, offset).wait_recv()
    ostage[...] = (
        pull_ref[theirs + z].astype(F32) + oland[0].astype(F32) + oland[1].astype(F32)
    ).astype(BF16)
    back_over(0).start()
    for sign in (1, -1):
        total = gathered(6 * sign, (5 * sign, 7 * sign))
        if sign > 0:
            back(8).wait_recv()
        mask = (1 - core if sign > 0 else core).astype(F32)
        pass_on(6 * sign, total + mask * zland[8].astype(F32))
    for offset in (2, -2, 4, -4):
        leaf(offset)
    core_sum(0, 0)
    core_sum(0, 1)
    for sign in (1, -1):
        pass_on(3 * sign, gathered(3 * sign, (2 * sign, 4 * sign, 6 * sign)))
    far = cland[0, 1 - line].astype(F32)
    for shift in (1, 2, 3):
        place_copy(shift).wait_recv()
        far = far + xland[shift - 1, 1 - line].astype(F32)
    hstage[...] = far.astype(BF16)
    line_copy = remote(hstage, hland, hsend.at[0], hrecv.at[0], across_line)
    line_copy.start()
    near = cland[0, line].astype(F32)
    for shift in (1, 2, 3):
        near = near + xland[shift - 1, line].astype(F32)
    wg_ref[...] = near

    sum_all = sland[z]
    for offset in range(1, NZ):
        pair = sland.at[along(-offset)]
        remote(pair, pair, qsend.at[offset], qrecv.at[offset], at_z(offset)).wait_recv()
        sum_all = sum_all + sland[along(-offset)]
    normed = (g_ref[mp].astype(F32) - average) * inverse
    pull = gathered(0, (1, -1, 3, -3))
    product = pull * normed
    turned = (product[:, :128] + product[:, 128:]).T
    gstage[0] = jnp.concatenate(
        [jnp.sum(turned, axis=0, keepdims=True), jnp.zeros((1, 128 - FEAT), F32)], axis=1
    )

    def gain_copy(stage, peer):
        src = gstage.at[min(stage, 1) if stage < 4 else 2]
        return remote(src, gland.at[stage], gsend.at[stage], grecv.at[stage], peer)

    gain_copy(0, mate).start()
    own_gain = gb_ref[mp].astype(F32)
    scaled = pull * jnp.concatenate([own_gain, own_gain], axis=1)
    ig_ref[...] = (
        inverse * (scaled - sum_all[0] * (1.0 / D) - normed * (sum_all[1] * (1.0 / D)))
    ).astype(BF16)
    gain_copy(0, mate).wait_recv()
    gstage[1] = gstage[0] + gland[0]
    for shift in (1, 2, 3):
        gain_copy(shift, at_dp(line, place_at(shift), core)).start()
    line_copy.wait_recv()
    wg_ref[...] += hland[...].astype(F32)
    gain_total = gstage[1]
    for shift in (1, 2, 3):
        gain_copy(shift, mate).wait_recv()
        gain_total = gain_total + gland[shift]
    gstage[2] = gain_total
    gain_copy(4, across_line).start()
    for which in (0, 1):
        other(which, 1).wait_send()
        back_other(which, 1 - 2 * which).wait_send()
    gain_over.wait_send()
    sums_over.wait_send()
    for offset in range(1, NZ):
        gain_to(offset).wait_send()
        sums_to(offset).wait_send()
    for offset in (1, 2, 3, 4, 5, 6, 7, 8, -1, -2, -3, -4, -5, -6, -7):
        spread(offset).wait_send()
        back(offset).wait_send()
        if abs(offset) > 1:
            over(offset).wait_send()
            back_over(offset).wait_send()
    over(0).wait_send()
    back_over(0).wait_send()
    for shift in shifts:
        core_copy(shift, 0).wait_send()
        core_copy(shift, 1).wait_send()
        if shift > 0:
            place_copy(shift).wait_send()
            gain_copy(shift, mate).wait_send()
    line_copy.wait_send()
    gain_copy(0, mate).wait_send()
    gain_copy(4, across_line).wait()
    gg_ref[...] = gain_total + gland[4]


def fused(x, gain, weights, out_grad):
    dma = pltpu.SemaphoreType.DMA
    return pl.pallas_call(
        fused_kernel,
        out_shape=(
            jax.ShapeDtypeStruct((PATCHES, HDIM), BF16),
            jax.ShapeDtypeStruct((FEAT, PATCHES), BF16),
            jax.ShapeDtypeStruct((ROWS, 3 * HDIM), F32),
            jax.ShapeDtypeStruct((1, 128), F32),
        ),
        in_specs=[
            pl.BlockSpec(memory_space=pl.ANY),
            pl.BlockSpec(memory_space=VMEM),
            pl.BlockSpec(memory_space=pl.ANY),
            pl.BlockSpec(memory_space=pl.ANY),
        ],
        out_specs=tuple([pl.BlockSpec(memory_space=VMEM)] * 4),
        scratch_shapes=[
            VMEM((D, 3 * HDIM), BF16),
            VMEM((PATCHES, HDIM), BF16),
            VMEM((NMP, FEAT, PATCHES), BF16),
            VMEM((NZ, NY, 1, 128), F32),
            VMEM((3 * HDIM, D), BF16),
            VMEM((NMP, 128), F32),
            VMEM((NMP, FEAT, 128), BF16),
            VMEM((NMP, FEAT, PATCHES), BF16),
            VMEM((3 * HDIM, PATCHES), BF16),
            VMEM((NMP, FEAT, PATCHES), BF16),
            VMEM((2 * CHIPS, ROWS, 3 * HDIM), BF16),
            VMEM((NZ, FEAT, PATCHES), BF16),
            VMEM((NZ, FEAT, PATCHES), BF16),
            VMEM((2, FEAT, PATCHES), BF16),
            VMEM((FEAT, PATCHES), BF16),
            VMEM((2, 1, PATCHES), F32),
            VMEM((2, 1, PATCHES), F32),
            VMEM((NZ, 2, 1, PATCHES), F32),
            VMEM((4, 2, ROWS, 3 * HDIM), BF16),
            VMEM((3, 2, ROWS, 3 * HDIM), BF16),
            VMEM((ROWS, 3 * HDIM), BF16),
            VMEM((ROWS, 3 * HDIM), BF16),
            VMEM((3, 1, 128), F32),
            VMEM((5, 1, 128), F32),
            dma((3,)),
            dma((NZ,)),
            dma((NZ,)),
            dma((NZ,)),
            dma((NZ,)),
            dma((2,)),
            dma((2,)),
            dma((NZ,)),
            dma((NZ,)),
            dma((2,)),
            dma((2,)),
            dma((NZ,)),
            dma((NZ,)),
            dma((NZ,)),
            dma((NZ,)),
            dma((NZ,)),
            dma((NZ,)),
            dma((2,)),
            dma((2,)),
            dma((8,)),
            dma((8,)),
            dma((3,)),
            dma((3,)),
            dma((1,)),
            dma((1,)),
            dma((5,)),
            dma((5,)),
        ],
        compiler_params=pltpu.CompilerParams(
            collective_id=0, has_side_effects=True, vmem_limit_bytes=56 << 20
        ),
    )(x, gain, weights, out_grad)


def on_device(tokens, gain, w_qkv, out_grad):
    attended, input_grad, weight_grad, gain_grad = fused(
        tokens.T, gain.reshape(1, FEAT), w_qkv[:, 0, :], out_grad
    )
    return attended, input_grad.T, weight_grad[:, None, :], gain_grad[0, :FEAT]


def solution(mesh):
    in_specs = (P("dp", "mp"), P("mp"), P(None, "mp", None), P("dp", "mp"))
    out_specs = (P("dp", "mp"), P("dp", "mp"), P("dp", "mp", None), P("mp"))
    return jax.shard_map(
        on_device, mesh=mesh, in_specs=in_specs, out_specs=out_specs, check_vma=False
    )
```

time: 1010 us -> 88.4 us (0.09)
  waiting for transfers between devices: 793 us -> 0 us
  blocking collectives: 170 us -> 0 us
  Pallas kernels: 0 us -> 80.5 us
  between operations: 13.9 us -> 0.64 us
  matrix products: 11.2 us -> 0 us
    reduce_scatter x2 -> x0, waiting for transfers between devices: 653 us -> none  [the longest x1 653 us: on_device(): lax.psum_scatter(lax.dot_general(weights, head_grad, (((1,), (1,)), ((),...]
    psum x3 -> x0, blocking collectives: 170 us -> none  [the longest x1 70.7 us: on_device(): lax.psum((jnp.sum(widened, axis=1), jnp.sum(widened * widened, axis=1)),...]
    all_gather x1 -> x0, waiting for transfers between devices: 141 us -> none  [on_device(): normed_in = lax.all_gather(normed_part, 'mp', axis=1, tiled=True)]
    pallas_call x0 -> x1, Pallas kernels: none -> 80.5 us  [fused(): pl.pallas_call(fused_kernel, out_shape=(jax.ShapeDtypeStruct((PATCHES, HD...]
    dot_general x10 -> x0, matrix products: 11.2 us -> none  [the longest x1 3.8 us: on_device(): lax.dot_general(normed_in, head_grad, (((0,), (0,)), ((), ())), preferred...]
  transfers between devices with their start and end apart: 3 -> 0, of which waited for: 2 -> 0; matrix products, arithmetic and copies ran while one was open for 1% -> 0% of each run, Pallas kernels for 0% -> 0%
where the time goes in v2:
time: 88.4 us; the launch traced here: 87.2 us
  Pallas kernels  80.5 us (91%)
  local copies, waits for them, and re-layouts  6.06 us (7%)
    pallas_call x1, Pallas kernels, fused(): pl.pallas_call(fused_kernel, out_shape=(jax.ShapeDtypeStruct((PATCHES, HD...  80.5 us
    unnamed x3, local copies, waits for them, and re-layouts  4.87 us

profile of v2, /device:TPU:1, one launch (start us, length us, event | category | flops | bytes accessed | tf_op | source)
XLA Modules:
  0.0 87.2 jit_solution(16490804070566965489)
XLA Ops:
  0.6 80.5 %shard_map.75 = (bf16[256,128]{1,0:T(8,128)(2,1)}, bf16[96,256]{1,0:T(8,128)(2,1)}, f32[192,384]{1,0:T(8,128)}, f32[1,128]{1,0:T(1,128)}) custom-call(bf16[96,256]{1,0:T(8,128)(2,1)} %bitcast.10, bf16[1,96]{1,0:T(2,128)(2,1)} %bitcast.11, bf16[3072,384]{1,0:T(8,128)(2,1)} %bitcast.7, bf16[256,128]{1,0:T(8,128)(2,1)} %do_any.1), custom_call_target="tpu_custom_call" | custom-call | tf_op jit(solution)/shard_map/pallas_call | solution.py:513
  81.1 1.2 %slice_bitcast_fusion = f32[96]{0:T(128)} fusion(f32[1,128]{1,0:T(1,128)} %get-tuple-element.11), kind=kLoop, calls=%fused_computation | loop fusion | bytes 768 | tf_op jit(solution)/shard_map/squeeze | solution.py:591
  82.3 2.0 %copy.8 = f32[192,1,384]{2,1,0:T(1,128)} copy(f32[192,1,384]{2,0,1:T(8,128)} %bitcast.8) | data formatting | bytes 589824
  84.3 1.5 %copy.11 = bf16[256,128]{1,0:T(8,128)(2,1)} copy(bf16[256,128]{1,0:T(8,128)(2,1)} %get-tuple-element.20) | data formatting | bytes 131072
  85.7 1.4 %copy.12 = bf16[256,96]{0,1:T(8,128)(2,1)} copy(bf16[256,96]{0,1:T(8,128)(2,1)} %bitcast.9) | data formatting | bytes 98304

commit v3 on v2

v3 whole, which is shorter than its diff:
```python
import math

import jax
import jax.numpy as jnp
from jax import lax
from jax.experimental import pallas as pl
from jax.experimental.pallas import tpu as pltpu
from jax.sharding import PartitionSpec as P

D = 3072
PATCHES = 256
HDIM = 128
FEAT = 96
NZ = 16
NY = 2
NMP = NZ * NY
CHIPS = 8
ROWS = 192
EPS = 1e-06
F32 = jnp.float32
BF16 = jnp.bfloat16
MESH = pl.DeviceIdType.MESH
VMEM = pltpu.VMEM


def remote(src, dst, send_sem, recv_sem, target):
    return pltpu.make_async_remote_copy(
        src_ref=src,
        dst_ref=dst,
        send_sem=send_sem,
        recv_sem=recv_sem,
        device_id=target,
        device_id_type=MESH,
    )


def folded(matrix):
    return jnp.sum(matrix.reshape(matrix.shape[0] // 8, 8, matrix.shape[1]), axis=0)


def column_mean(matrix):
    return jnp.sum(matrix, axis=0, keepdims=True) * (1.0 / matrix.shape[0])


def unit_columns(matrix):
    centred = matrix - column_mean(matrix)
    inverse = lax.rsqrt(column_mean(centred * centred) + EPS)
    return centred * inverse, inverse


def unit_pullback(normal, inverse, cotangent):
    return inverse * (
        cotangent - column_mean(cotangent) - normal * column_mean(cotangent * normal)
    )


def dot(a, b):
    return jnp.dot(a, b, preferred_element_type=F32)


def dot_rows(a, b):
    return lax.dot_general(a, b, (((1,), (1,)), ((), ())), preferred_element_type=F32)


def hub_of(offset):
    sign = 1 if offset > 0 else -1
    return sign * {1: 0, 3: 0, 2: 3, 4: 3, 6: 3, 5: 6, 7: 6}[abs(offset)]


FAR = (5, -5, 7, -7, 8)
NEAR = (2, -2, 4, -4)


def fused_kernel(
    x_any,
    gain_ref,
    w_any,
    do_any,
    att_ref,
    ig_ref,
    wg_ref,
    gg_ref,
    w_ref,
    do_ref,
    g_ref,
    gains,
    wt_ref,
    rows_ref,
    gb_ref,
    nt_ref,
    hg_ref,
    hgt_ref,
    pull_ref,
    ws_ref,
    zland,
    yland,
    oland,
    sums,
    spair,
    sland,
    spart,
    cland,
    xland,
    hland,
    hstage,
    gstage,
    gland,
    local,
    zsend,
    zrecv,
    ysend,
    yrecv,
    osend,
    orecv,
    ssend,
    srecv,
    psend,
    precv,
    rzsend,
    rzrecv,
    rysend,
    ryrecv,
    rosend,
    rorecv,
    csend,
    crecv,
    xsend,
    xrecv,
    hsend,
    hrecv,
    gsend,
    grecv,
):
    mp = lax.axis_index("mp")
    row, z = mp // NZ, mp % NZ
    dp = lax.axis_index("dp")
    line, place, core = dp // 8, (dp // 2) % 4, dp % 2
    sign8 = 1 - 2 * core
    mine, theirs = row * NZ, (1 - row) * NZ
    partner = {"mp": theirs + z}

    def along(offset):
        return (z + offset + 2 * NZ) % NZ

    def at_z(offset):
        return {"mp": mine + along(offset)}

    def at_dp(lines, places, cores):
        return {"dp": (((line + lines) % 2) * 4 + place_at(places)) * 2 + (core + cores) % 2}

    def place_at(shift):
        return (place + shift) % 4

    def hub(offset):
        return 6 * sign8 if offset == 8 else hub_of(offset)

    mate = at_dp(0, 0, 1)
    across_line = at_dp(1, 0, 0)
    others = [(i, j, k) for i in (0, 1) for j in range(4) for k in (0, 1) if i + j + k > 0]

    own_copy = pltpu.make_async_copy(x_any, g_ref.at[mp], local.at[0])
    w_copy = pltpu.make_async_copy(w_any, w_ref, local.at[1])
    do_copy = pltpu.make_async_copy(do_any, do_ref, local.at[2])
    own_copy.start()
    barrier = pltpu.get_barrier_semaphore()
    peers = [at_z(offset) for offset in (3, -3, 2, -2, 1, -1)] + [partner]
    peers += [at_dp(*steps) for steps in others]
    for peer in peers:
        pl.semaphore_signal(barrier, inc=1, device_id=peer, device_id_type=MESH)
    w_copy.start()
    do_copy.start()
    gains[mp] = jnp.concatenate(
        [gain_ref[...].astype(F32), jnp.zeros((1, 128 - FEAT), F32)], axis=1
    )
    own_copy.wait()
    pl.semaphore_wait(barrier, len(peers))

    class Both:
        def __init__(self, block, send, recv, offset, target):
            slot = offset % NZ
            self.copies = [
                remote(ref.at[block], ref.at[block], send.at[i, slot], recv.at[i, slot], target)
                for i, ref in enumerate((g_ref, gains))
            ]

        def start(self):
            for copy in self.copies:
                copy.start()

        def wait_send(self):
            for copy in self.copies:
                copy.wait_send()

        def wait_recv(self):
            for copy in self.copies:
                copy.wait_recv()

    def spread(offset):
        block = mine + along(-hub(offset))
        return Both(block, zsend, zrecv, offset, at_z(offset - hub(offset)))

    def arrived(offset):
        Both(mine + along(-offset), zsend, zrecv, offset, at_z(1)).wait_recv()

    def over(offset):
        return Both(mine + along(-offset), ysend, yrecv, offset, partner)

    def over_arrived(offset):
        Both(theirs + along(-offset), ysend, yrecv, offset, partner).wait_recv()

    def other(offset):
        block = theirs + along(-hub(offset))
        return Both(block, osend, orecv, offset, at_z(offset - hub(offset)))

    def other_arrived(offset):
        Both(theirs + along(-offset), osend, orecv, offset, at_z(1)).wait_recv()

    for offset in (3, -3):
        spread(offset).start()
    over(0).start()
    for offset in (1, -1):
        spread(offset).start()
    w_copy.wait()
    for part in range(D // 256):
        wt_ref[:, part * 256 : (part + 1) * 256] = w_ref[part * 256 : (part + 1) * 256, :].T
    do_copy.wait()
    cotangent = do_ref[...].T
    for sign in (1, -1):
        arrived(3 * sign)
        for offset in (6 * sign, 4 * sign, 2 * sign):
            spread(offset).start()
        over(3 * sign).start()
    for offset in (1, -1, 2, -2, 4, -4):
        arrived(offset)
        over(offset).start()
    for sign in (1, -1):
        arrived(6 * sign)
        over(6 * sign).start()
        for offset in (5 * sign, 7 * sign):
            spread(offset).start()
    spread(8).start()
    for sign in (1, -1):
        over_arrived(6 * sign)
        for offset in (5 * sign, 7 * sign):
            other(offset).start()
    other(8).start()
    for offset in FAR:
        arrived(offset)

    shift_row = jnp.sum(g_ref[mp].astype(F32), axis=0, keepdims=True) * (1.0 / FEAT)

    def add_block(block, totals):
        moved = g_ref[block].astype(F32) - shift_row
        return totals[0] + folded(moved), totals[1] + folded(moved * moved)

    def gain_columns(start):
        for i in range(NZ):
            rows_ref[i : i + 1, :] = gains[start + i]
        turned = rows_ref[...].T
        for i in range(NZ):
            gb_ref[start + i] = jnp.broadcast_to(turned[:FEAT, i : i + 1], (FEAT, 128)).astype(BF16)

    def gain_product(start):
        half = NZ * FEAT
        columns = pl.ds(pl.multiple_of(start * FEAT, half), half)
        return dot(wt_ref[:, columns], gb_ref[pl.ds(start, NZ)].reshape(half, 128))

    zero = jnp.zeros((8, PATCHES), F32)
    totals = lax.fori_loop(mine, mine + NZ, add_block, (zero, zero))
    gain_columns(mine)
    gain_weights = gain_product(mine)
    for offset in (0, 3, -3, 1, -1, 2, -2, 4, -4):
        over_arrived(offset)
    for offset in FAR:
        other_arrived(offset)
    gain_columns(theirs)
    totals = lax.fori_loop(theirs, theirs + NZ, add_block, totals)
    first = jnp.sum(totals[0], axis=0, keepdims=True) * (1.0 / D)
    second = jnp.sum(totals[1], axis=0, keepdims=True) * (1.0 / D)
    average = shift_row + first
    inverse = lax.rsqrt(second - first * first + EPS)

    def normalize(block, carry):
        factor = gb_ref[block].astype(F32)
        factor = jnp.concatenate([factor, factor], axis=1)
        normed = (g_ref[block].astype(F32) - average) * inverse
        nt_ref[block] = (normed * factor).astype(BF16)
        return carry

    lax.fori_loop(0, NMP, normalize, 0)

    wide = dot(wt_ref[...], nt_ref[...].reshape(D, PATCHES))
    projected = wide.astype(BF16)
    query, query_inverse = unit_columns(projected[:HDIM].astype(F32))
    keys, keys_inverse = unit_columns(projected[HDIM : 2 * HDIM].astype(F32))
    values = projected[2 * HDIM :]
    query_r, keys_r = query.astype(BF16), keys.astype(BF16)
    scale = 1.0 / math.sqrt(HDIM)
    exponent = jnp.exp(dot(keys_r.T, query_r) * scale)
    soft = exponent / jnp.sum(exponent, axis=0, keepdims=True)
    soft_r = soft.astype(BF16)
    soft_grad = dot(values.T, cotangent)
    values_grad = dot_rows(cotangent, soft_r)
    score_grad = soft * (soft_grad - jnp.sum(soft * soft_grad, axis=0, keepdims=True))
    score_grad = (score_grad * scale).astype(BF16)
    query_grad = unit_pullback(query, query_inverse, dot(keys_r, score_grad))
    keys_grad = unit_pullback(keys, keys_inverse, dot_rows(query_r, score_grad))
    hg = jnp.concatenate([query_grad, keys_grad, values_grad], axis=0).astype(BF16)
    hg_ref[...] = hg

    def pull_rows(start):
        def pull_part(part, carry):
            block = start + part * 8
            rows = pl.ds(pl.multiple_of(block * FEAT, 8 * FEAT), 8 * FEAT)
            pull_ref[pl.ds(block, 8)] = (
                dot(w_ref[rows, :], hg_ref[...]).astype(BF16).reshape(8, FEAT, PATCHES)
            )
            return carry

        lax.fori_loop(0, 2, pull_part, 0)

    def back_over(offset):
        slot = offset % NZ
        src = pull_ref.at[theirs + along(-offset)]
        return remote(src, yland.at[slot], rysend.at[slot], ryrecv.at[slot], partner)

    def back_along(start, land, send, recv, offset):
        slot = offset % NZ
        return remote(
            pull_ref.at[start + along(-offset)],
            land.at[slot],
            send.at[slot],
            recv.at[slot],
            at_z(hub(offset) - offset),
        )

    def back_other(offset):
        return back_along(theirs, oland, rosend, rorecv, offset)

    def back(offset):
        return back_along(mine, zland, rzsend, rzrecv, offset)

    def back_sums(offset, src):
        slot = offset % NZ
        return remote(
            src, sland.at[slot], ssend.at[slot], srecv.at[slot], at_z(hub(offset) - offset)
        )

    def landed(copy, land, offset):
        copy(offset).wait_recv()
        return land[offset % NZ].astype(F32)

    pull_rows(theirs)
    for offset in FAR:
        back_other(offset).start()
    pull_rows(mine)
    for offset in FAR:
        back(offset).start()
    gain_weights = gain_weights + gain_product(theirs)
    hg_wide = hg.astype(F32)
    factor = jnp.concatenate([gain_weights, gain_weights], axis=1)
    sums[0] = jnp.sum(hg_wide * factor, axis=0, keepdims=True)
    sums[1] = jnp.sum(hg_wide * wide, axis=0, keepdims=True)
    sums_over = remote(sums, spair, psend.at[0], precv.at[0], partner)
    sums_over.start()
    for offset in NEAR + (3, -3):
        back_over(offset).start()

    def core_copy(shift, line_of):
        chip = line_of * 4 + place_at(shift)
        slot = shift * 2 + line_of
        return remote(
            ws_ref.at[chip * 2 + 1 - core],
            cland.at[shift, line_of],
            csend.at[slot],
            crecv.at[slot],
            mate,
        )

    def core_sum(shift, line_of):
        chip = line_of * 4 + place_at(shift)
        core_copy(shift, line_of).wait_recv()
        both = cland[shift, line_of].astype(F32) + ws_ref[chip * 2 + core].astype(F32)
        cland[shift, line_of] = both.astype(BF16)

    def place_copy(shift):
        return remote(
            cland.at[shift],
            xland.at[shift - 1],
            xsend.at[shift - 1],
            xrecv.at[shift - 1],
            at_dp(0, shift, 0),
        )

    hgt_ref[...] = hg.T
    shifts = (2, 1, 3, 0)
    for shift in shifts:
        for line_of in (0, 1):
            chip = line_of * 4 + place_at(shift)
            block = dot(nt_ref[pl.ds(chip * 4, 4)].reshape(4 * FEAT, PATCHES), hgt_ref[...])
            ws_ref[pl.ds(chip * 2, 2)] = block.astype(BF16).reshape(2, ROWS, 3 * HDIM)
            core_copy(shift, line_of).start()
    att_ref[...] = dot(values, soft_r).T.astype(BF16)
    sums_over.wait_recv()
    spair[...] = spair[...] + sums[...]
    for offset in FAR + NEAR + (1, -1):
        back_sums(offset, spair).start()

    for sign in (1, -1):
        total = pull_ref[theirs + along(-6 * sign)].astype(F32)
        total = total + landed(back_other, oland, 5 * sign) + landed(back_other, oland, 7 * sign)
        if sign > 0:
            back_other(8).wait_recv()
        mask = (1 - core if sign > 0 else core).astype(F32)
        total = total + mask * oland[8].astype(F32)
        pull_ref[theirs + along(-6 * sign)] = total.astype(BF16)
        back_over(6 * sign).start()
    for offset in (1, -1, 0):
        back_over(offset).start()
    for shift in shifts[:-1]:
        core_sum(shift, 0)
        core_sum(shift, 1)
        place_copy(shift).start()

    def gathered(offset, inputs):
        total = pull_ref[mine + along(-offset)].astype(F32) + landed(back_over, yland, offset)
        for at in inputs:
            total = total + landed(back, zland, at)
        return total

    def pass_on(offset, total):
        pull_ref[mine + along(-offset)] = total.astype(BF16)
        back(offset).start()

    def sums_of(inputs):
        total = spair[...]
        for at in inputs:
            back_sums(at, spair).wait_recv()
            total = total + sland[at % NZ]
        return total

    for offset in NEAR:
        pass_on(offset, gathered(offset, ()))
    for sign in (1, -1):
        total = gathered(6 * sign, (5 * sign, 7 * sign))
        if sign > 0:
            back(8).wait_recv()
        mask = (1 - core if sign > 0 else core).astype(F32)
        pass_on(6 * sign, total + mask * zland[8].astype(F32))
    for which, sign in enumerate((1, -1)):
        if sign > 0:
            back_sums(8, spair).wait_recv()
        mask = (1 - core if sign > 0 else core).astype(F32)
        spart[which] = sums_of((5 * sign, 7 * sign)) + mask * sland[8]
        back_sums(6 * sign, spart.at[which]).start()
    for offset in (1, -1):
        pass_on(offset, gathered(offset, ()))
    core_sum(0, 0)
    core_sum(0, 1)
    for sign in (1, -1):
        pass_on(3 * sign, gathered(3 * sign, (2 * sign, 4 * sign, 6 * sign)))
    for which, sign in enumerate((1, -1)):
        spart[2 + which] = sums_of((2 * sign, 4 * sign, 6 * sign))
        back_sums(3 * sign, spart.at[2 + which]).start()
    far = cland[0, 1 - line].astype(F32)
    for shift in (1, 2, 3):
        place_copy(shift).wait_recv()
        far = far + xland[shift - 1, 1 - line].astype(F32)
    hstage[...] = far.astype(BF16)
    line_copy = remote(hstage, hland, hsend.at[0], hrecv.at[0], across_line)
    line_copy.start()
    near = cland[0, line].astype(F32)
    for shift in (1, 2, 3):
        near = near + xland[shift - 1, line].astype(F32)
    wg_ref[...] = near

    normed = (g_ref[mp].astype(F32) - average) * inverse
    pull = gathered(0, (1, -1, 3, -3))
    product = pull * normed
    turned = (product[:, :128] + product[:, 128:]).T
    gstage[...] = jnp.concatenate(
        [jnp.sum(turned, axis=0, keepdims=True), jnp.zeros((1, 128 - FEAT), F32)], axis=1
    )

    def gain_copy(steps):
        slot = steps[0] * 8 + steps[1] * 2 + steps[2]
        return remote(gstage, gland.at[slot], gsend.at[slot], grecv.at[slot], at_dp(*steps))

    for steps in others:
        gain_copy(steps).start()
    sum_all = sums_of((1, -1, 3, -3))
    own_gain = gb_ref[mp].astype(F32)
    scaled = pull * jnp.concatenate([own_gain, own_gain], axis=1)
    ig_ref[...] = (
        inverse * (scaled - sum_all[0] * (1.0 / D) - normed * (sum_all[1] * (1.0 / D)))
    ).astype(BF16)
    line_copy.wait_recv()
    wg_ref[...] += hland[...].astype(F32)
    sums_over.wait_send()
    for offset in (1, 2, 3, 4, 5, 6, 7, 8, -1, -2, -3, -4, -5, -6, -7):
        spread(offset).wait_send()
        back(offset).wait_send()
        back_sums(offset, spair).wait_send()
        if offset in FAR:
            other(offset).wait_send()
            back_other(offset).wait_send()
        else:
            over(offset).wait_send()
            back_over(offset).wait_send()
    over(0).wait_send()
    back_over(0).wait_send()
    for shift in shifts:
        core_copy(shift, 0).wait_send()
        core_copy(shift, 1).wait_send()
        if shift > 0:
            place_copy(shift).wait_send()
    line_copy.wait_send()
    gain_total = gstage[...]
    for steps in others:
        gain_copy(steps).wait()
        gain_total = gain_total + gland[steps[0] * 8 + steps[1] * 2 + steps[2]]
    gg_ref[...] = gain_total


def fused(x, gain, weights, out_grad):
    dma = pltpu.SemaphoreType.DMA
    return pl.pallas_call(
        fused_kernel,
        out_shape=(
            jax.ShapeDtypeStruct((PATCHES, HDIM), BF16),
            jax.ShapeDtypeStruct((FEAT, PATCHES), BF16),
            jax.ShapeDtypeStruct((ROWS, 3 * HDIM), F32),
            jax.ShapeDtypeStruct((1, 128), F32),
        ),
        in_specs=[
            pl.BlockSpec(memory_space=pltpu.HBM),
            pl.BlockSpec(memory_space=VMEM),
            pl.BlockSpec(memory_space=pltpu.HBM),
            pl.BlockSpec(memory_space=pltpu.HBM),
        ],
        out_specs=tuple([pl.BlockSpec(memory_space=VMEM)] * 4),
        scratch_shapes=[
            VMEM((D, 3 * HDIM), BF16),
            VMEM((PATCHES, HDIM), BF16),
            VMEM((NMP, FEAT, PATCHES), BF16),
            VMEM((NMP, 1, 128), F32),
            VMEM((3 * HDIM, D), BF16),
            VMEM((NZ, 128), F32),
            VMEM((NMP, FEAT, 128), BF16),
            VMEM((NMP, FEAT, PATCHES), BF16),
            VMEM((3 * HDIM, PATCHES), BF16),
            VMEM((PATCHES, 3 * HDIM), BF16),
            VMEM((NMP, FEAT, PATCHES), BF16),
            VMEM((2 * CHIPS, ROWS, 3 * HDIM), BF16),
            VMEM((NZ, FEAT, PATCHES), BF16),
            VMEM((NZ, FEAT, PATCHES), BF16),
            VMEM((NZ, FEAT, PATCHES), BF16),
            VMEM((2, 1, PATCHES), F32),
            VMEM((2, 1, PATCHES), F32),
            VMEM((NZ, 2, 1, PATCHES), F32),
            VMEM((4, 2, 1, PATCHES), F32),
            VMEM((4, 2, ROWS, 3 * HDIM), BF16),
            VMEM((3, 2, ROWS, 3 * HDIM), BF16),
            VMEM((ROWS, 3 * HDIM), BF16),
            VMEM((ROWS, 3 * HDIM), BF16),
            VMEM((1, 128), F32),
            VMEM((2 * CHIPS, 1, 128), F32),
            dma((3,)),
            dma((2, NZ)),
            dma((2, NZ)),
            dma((2, NZ)),
            dma((2, NZ)),
            dma((2, NZ)),
            dma((2, NZ)),
            dma((NZ,)),
            dma((NZ,)),
            dma((1,)),
            dma((1,)),
            dma((NZ,)),
            dma((NZ,)),
            dma((NZ,)),
            dma((NZ,)),
            dma((NZ,)),
            dma((NZ,)),
            dma((8,)),
            dma((8,)),
            dma((3,)),
            dma((3,)),
            dma((1,)),
            dma((1,)),
            dma((2 * CHIPS,)),
            dma((2 * CHIPS,)),
        ],
        compiler_params=pltpu.CompilerParams(
            collective_id=0, has_side_effects=True, vmem_limit_bytes=28 << 20
        ),
    )(x, gain, weights, out_grad)


def on_device(tokens, gain, w_qkv, out_grad):
    attended, input_grad, weight_grad, gain_grad = fused(
        tokens.T, gain.reshape(1, FEAT), w_qkv[:, 0, :], out_grad
    )
    return attended, input_grad.T, weight_grad[:, None, :], gain_grad[0, :FEAT]


def solution(mesh):
    in_specs = (P("dp", "mp"), P("mp"), P(None, "mp", None), P("dp", "mp"))
    out_specs = (P("dp", "mp"), P("dp", "mp"), P("dp", "mp", None), P("mp"))
    return jax.shard_map(
        on_device, mesh=mesh, in_specs=in_specs, out_specs=out_specs, check_vma=False
    )
```

time: 88.4 us -> 79.7 us (0.902); the launches traced: 87.2 us -> 79.4 us
  Pallas kernels: 80.5 us -> 72 us
    pallas_call x1, Pallas kernels: 80.5 us -> 72 us  [fused(): pl.pallas_call(fused_kernel, out_shape=(jax.ShapeDtypeStruct((PATCHES, HD...]
    unnamed x3 -> x11, local copies, waits for them, and re-layouts: 4.87 us -> 6.22 us
where the time goes in v3:
time: 79.7 us; the launch traced here: 79.4 us
  Pallas kernels  72 us (90%)
  local copies, waits for them, and re-layouts  6.73 us (8%)
    pallas_call x1, Pallas kernels, fused(): pl.pallas_call(fused_kernel, out_shape=(jax.ShapeDtypeStruct((PATCHES, HD...  72 us
    unnamed x11, local copies, waits for them, and re-layouts  6.22 us

profile of v3, /device:TPU:1, one launch (start us, length us, event | category | flops | bytes accessed | tf_op | source)
XLA Modules:
  0.0 79.4 jit_solution(15880490526615214047)
XLA Ops:
  0.6 0.0 copy-start
  0.6 1.7 %copy-done = bf16[3072,1,384]{2,0,1:T(8,128)(2,1)S(1)} copy-done((bf16[3072,1,384]{2,0,1:T(8,128)(2,1)S(1)}, bf16[3072,1,384]{2,0,1:T(8,128)(2,1)}, u32[]{:S(2)}) %copy-start) | copy-done | bytes 2359320
  2.3 0.0 copy-start.1
  2.3 0.8 %copy-done.1 = bf16[256,128]{1,0:T(8,128)(2,1)S(1)} copy-done((bf16[256,128]{1,0:T(8,128)(2,1)S(1)}, bf16[256,128]{1,0:T(8,128)(2,1)}, u32[]{:S(2)}) %copy-start.1) | copy-done | bytes 65560
  3.1 0.0 copy-start.2
  3.1 0.8 %copy-done.2 = bf16[256,96]{0,1:T(8,128)(2,1)S(1)} copy-done((bf16[256,96]{0,1:T(8,128)(2,1)S(1)}, bf16[256,96]{0,1:T(8,128)(2,1)}, u32[]{:S(2)}) %copy-start.2) | copy-done | bytes 49176
  3.9 0.0 copy-start.3
  3.9 0.7 copy-done.3
  4.6 72.0 %shard_map.75 = (bf16[256,128]{1,0:T(8,128)(2,1)S(1)}, bf16[96,256]{1,0:T(8,128)(2,1)S(1)}, f32[192,384]{1,0:T(8,128)S(1)}, f32[1,128]{1,0:T(1,128)S(1)}) custom-call(bf16[96,256]{1,0:T(8,128)(2,1)S(1)} %bitcast.10, bf16[1,96]{1,0:T(2,128)(2,1)S(1)} %bitcast.11, bf16[3072,384]{1,0:T(8,128)(2,1)S(1)} %bitcast.7, bf16[256,128]{1,0:T(8,128)(2,1)S(1)} %copy-done.1), custom_call_target="tpu_custom_call" | custom-call | tf_op jit(solution)/shard_map/pallas_call | solution.py:527
  76.7 0.5 slice_bitcast_fusion
  77.2 1.0 %copy.8 = f32[192,1,384]{2,1,0:T(1,128)} copy(f32[192,1,384]{2,0,1:T(8,128)S(1)} %bitcast.8) | data formatting | bytes 589824
  78.2 0.6 copy.11
  78.8 0.6 copy.12
Async XLA Ops:
  0.6 1.7 %copy-start = (bf16[3072,1,384]{2,0,1:T(8,128)(2,1)S(1)}, bf16[3072,1,384]{2,0,1:T(8,128)(2,1)}, u32[]{:S(2)}) copy-start(bf16[3072,1,384]{2,0,1:T(8,128)(2,1)} %param.6) | copy-start | bytes 7077892
  2.3 0.8 %copy-start.1 = (bf16[256,128]{1,0:T(8,128)(2,1)S(1)}, bf16[256,128]{1,0:T(8,128)(2,1)}, u32[]{:S(2)}) copy-start(bf16[256,128]{1,0:T(8,128)(2,1)} %do_any.1) | copy-start | bytes 196612
  3.1 0.8 %copy-start.2 = (bf16[256,96]{0,1:T(8,128)(2,1)S(1)}, bf16[256,96]{0,1:T(8,128)(2,1)}, u32[]{:S(2)}) copy-start(bf16[256,96]{0,1:T(8,128)(2,1)} %param.4) | copy-start | bytes 147460
  3.9 0.7 copy-start.3

commit v4 on v3

--- a/solution.py
+++ b/solution.py
@@ -68,7 +68,21 @@
 
 
 FAR = (5, -5, 7, -7, 8)
+FIVES = (5, -5)
 NEAR = (2, -2, 4, -4)
+GATHER_SLOTS = (
+    *(("z", offset) for offset in (3, -3, 1, -1, 6, -6) + NEAR),
+    *(("y", offset) for offset in (6, -6)),
+    "z far",
+    "y near",
+    "other",
+)
+SCATTER_SLOTS = (
+    *(("z", offset) for offset in NEAR + (6, -6, 3, -3, 1, -1)),
+    *(("y", offset) for offset in (8, 7, -7, 6, -6, 3, -3, 1, -1, 0) + NEAR),
+    "z far",
+    "other",
+)
 
 
 def fused_kernel(
@@ -76,10 +90,13 @@
     gain_ref,
     w_any,
     do_any,
+    att_any,
+    ig_any,
+    wg_any,
+    gg_ref,
     att_ref,
     ig_ref,
     wg_ref,
-    gg_ref,
     w_ref,
     do_ref,
     g_ref,
@@ -100,28 +117,19 @@
     sland,
     spart,
     cland,
+    mland,
     xland,
     hland,
     hstage,
     gstage,
     gland,
     local,
-    zsend,
-    zrecv,
-    ysend,
-    yrecv,
-    osend,
-    orecv,
+    bsend,
+    brecv,
+    rsend,
+    rrecv,
     ssend,
     srecv,
-    psend,
-    precv,
-    rzsend,
-    rzrecv,
-    rysend,
-    ryrecv,
-    rosend,
-    rorecv,
     csend,
     crecv,
     xsend,
@@ -176,10 +184,11 @@
     pl.semaphore_wait(barrier, len(peers))
 
     class Both:
-        def __init__(self, block, send, recv, offset, target):
-            slot = offset % NZ
+        def __init__(self, key, target, block, count=1):
+            slot = GATHER_SLOTS.index(key)
+            part = block if count == 1 else pl.ds(block, count)
             self.copies = [
-                remote(ref.at[block], ref.at[block], send.at[i, slot], recv.at[i, slot], target)
+                remote(ref.at[part], ref.at[part], bsend.at[i], brecv.at[i, slot], target)
                 for i, ref in enumerate((g_ref, gains))
             ]
 
@@ -196,24 +205,24 @@
                 copy.wait_recv()
 
     def spread(offset):
-        block = mine + along(-hub(offset))
-        return Both(block, zsend, zrecv, offset, at_z(offset - hub(offset)))
+        key = "z far" if offset in FAR else ("z", offset)
+        return Both(key, at_z(offset - hub(offset)), mine + along(-hub(offset)))
 
     def arrived(offset):
-        Both(mine + along(-offset), zsend, zrecv, offset, at_z(1)).wait_recv()
+        Both(("z", offset), at_z(1), mine + along(-offset)).wait_recv()
 
     def over(offset):
-        return Both(mine + along(-offset), ysend, yrecv, offset, partner)
+        key = ("y", offset) if abs(offset) == 6 else "y near"
+        return Both(key, partner, mine + along(-offset))
 
     def over_arrived(offset):
-        Both(theirs + along(-offset), ysend, yrecv, offset, partner).wait_recv()
+        Both(("y", offset), partner, theirs + along(-offset)).wait_recv()
 
     def other(offset):
-        block = theirs + along(-hub(offset))
-        return Both(block, osend, orecv, offset, at_z(offset - hub(offset)))
-
-    def other_arrived(offset):
-        Both(theirs + along(-offset), osend, orecv, offset, at_z(1)).wait_recv()
+        return Both("other", at_z(offset - hub(offset)), theirs + along(-hub(offset)))
+
+    def all_arrived(key, count):
+        Both(key, partner, 0, count).wait_recv()
 
     for offset in (3, -3):
         spread(offset).start()
@@ -230,7 +239,7 @@
         for offset in (6 * sign, 4 * sign, 2 * sign):
             spread(offset).start()
         over(3 * sign).start()
-    for offset in (1, -1, 2, -2, 4, -4):
+    for offset in (1, -1):
         arrived(offset)
         over(offset).start()
     for sign in (1, -1):
@@ -239,13 +248,15 @@
         for offset in (5 * sign, 7 * sign):
             spread(offset).start()
     spread(8).start()
+    for offset in NEAR:
+        arrived(offset)
+        over(offset).start()
     for sign in (1, -1):
         over_arrived(6 * sign)
         for offset in (5 * sign, 7 * sign):
             other(offset).start()
     other(8).start()
-    for offset in FAR:
-        arrived(offset)
+    all_arrived("z far", len(FAR))
 
     shift_row = jnp.sum(g_ref[mp].astype(F32), axis=0, keepdims=True) * (1.0 / FEAT)
 
@@ -269,10 +280,8 @@
     totals = lax.fori_loop(mine, mine + NZ, add_block, (zero, zero))
     gain_columns(mine)
     gain_weights = gain_product(mine)
-    for offset in (0, 3, -3, 1, -1, 2, -2, 4, -4):
-        over_arrived(offset)
-    for offset in FAR:
-        other_arrived(offset)
+    all_arrived("y near", 9)
+    all_arrived("other", len(FAR))
     gain_columns(theirs)
     totals = lax.fori_loop(theirs, theirs + NZ, add_block, totals)
     first = jnp.sum(totals[0], axis=0, keepdims=True) * (1.0 / D)
@@ -319,52 +328,69 @@
 
         lax.fori_loop(0, 2, pull_part, 0)
 
+    def scatter_copy(key, src, dst, target):
+        return remote(src, dst, rsend.at[0], rrecv.at[SCATTER_SLOTS.index(key)], target)
+
     def back_over(offset):
-        slot = offset % NZ
         src = pull_ref.at[theirs + along(-offset)]
-        return remote(src, yland.at[slot], rysend.at[slot], ryrecv.at[slot], partner)
-
-    def back_along(start, land, send, recv, offset):
-        slot = offset % NZ
+        return scatter_copy(("y", offset), src, yland.at[offset % NZ], partner)
+
+    def back_other(offset):
+        src = pull_ref.at[theirs + along(-offset)]
+        return scatter_copy("other", src, oland.at[FIVES.index(offset)], at_z(hub(offset) - offset))
+
+    def back(offset):
+        key = "z far" if offset in FAR else ("z", offset)
+        src = pull_ref.at[mine + along(-offset)]
+        return scatter_copy(key, src, zland.at[offset % NZ], at_z(hub(offset) - offset))
+
+    def all_landed(key, land, count):
+        part = land.at[pl.ds(0, count)]
+        scatter_copy(key, part, part, partner).wait_recv()
+
+    def back_sums(offset, src):
+        stage = 0 if offset in FAR else (2 if abs(offset) in (1, 3) else 1)
         return remote(
-            pull_ref.at[start + along(-offset)],
-            land.at[slot],
-            send.at[slot],
-            recv.at[slot],
+            src,
+            sland.at[offset % NZ],
+            ssend.at[0],
+            srecv.at[stage],
             at_z(hub(offset) - offset),
         )
 
-    def back_other(offset):
-        return back_along(theirs, oland, rosend, rorecv, offset)
-
-    def back(offset):
-        return back_along(mine, zland, rzsend, rzrecv, offset)
-
-    def back_sums(offset, src):
-        slot = offset % NZ
-        return remote(
-            src, sland.at[slot], ssend.at[slot], srecv.at[slot], at_z(hub(offset) - offset)
-        )
+    def sums_landed(stage, count):
+        part = sland.at[pl.ds(0, count)]
+        remote(part, part, ssend.at[0], srecv.at[stage], partner).wait_recv()
 
     def landed(copy, land, offset):
         copy(offset).wait_recv()
         return land[offset % NZ].astype(F32)
 
+    def gathered(offset, inputs):
+        total = pull_ref[mine + along(-offset)].astype(F32) + landed(back_over, yland, offset)
+        for at in inputs:
+            total = total + landed(back, zland, at)
+        return total
+
+    def pass_on(offset, total):
+        pull_ref[mine + along(-offset)] = total.astype(BF16)
+        back(offset).start()
+
     pull_rows(theirs)
-    for offset in FAR:
+    for offset in FIVES:
         back_other(offset).start()
+    for offset in (8, 7, -7):
+        back_over(offset).start()
     pull_rows(mine)
-    for offset in FAR:
+    for offset in FIVES:
         back(offset).start()
     gain_weights = gain_weights + gain_product(theirs)
     hg_wide = hg.astype(F32)
     factor = jnp.concatenate([gain_weights, gain_weights], axis=1)
     sums[0] = jnp.sum(hg_wide * factor, axis=0, keepdims=True)
     sums[1] = jnp.sum(hg_wide * wide, axis=0, keepdims=True)
-    sums_over = remote(sums, spair, psend.at[0], precv.at[0], partner)
+    sums_over = remote(sums, spair, ssend.at[1], srecv.at[3], partner)
     sums_over.start()
-    for offset in NEAR + (3, -3):
-        back_over(offset).start()
 
     def core_copy(shift, line_of):
         chip = line_of * 4 + place_at(shift)
@@ -372,7 +398,7 @@
         return remote(
             ws_ref.at[chip * 2 + 1 - core],
             cland.at[shift, line_of],
-            csend.at[slot],
+            csend.at[0],
             crecv.at[slot],
             mate,
         )
@@ -383,95 +409,104 @@
         both = cland[shift, line_of].astype(F32) + ws_ref[chip * 2 + core].astype(F32)
         cland[shift, line_of] = both.astype(BF16)
 
-    def place_copy(shift):
+    def place_copy(shift, line_of):
+        up = shift == 1 or (shift == 2 and line_of == 0)
+        land = mland.at[line_of] if shift == 2 else xland.at[0 if up else 1, line_of]
         return remote(
-            cland.at[shift],
-            xland.at[shift - 1],
-            xsend.at[shift - 1],
-            xrecv.at[shift - 1],
-            at_dp(0, shift, 0),
+            cland.at[shift, line_of],
+            land,
+            xsend.at[0],
+            xrecv.at[shift * 2 - 2 + line_of],
+            at_dp(0, 1 if up else 3, 0),
         )
 
+    def merge(shift, line_of):
+        place_copy(2, line_of).wait_recv()
+        both = cland[shift, line_of].astype(F32) + mland[line_of].astype(F32)
+        cland[shift, line_of] = both.astype(BF16)
+        place_copy(shift, line_of).start()
+
     hgt_ref[...] = hg.T
-    shifts = (2, 1, 3, 0)
-    for shift in shifts:
+
+    def share(shift):
         for line_of in (0, 1):
             chip = line_of * 4 + place_at(shift)
             block = dot(nt_ref[pl.ds(chip * 4, 4)].reshape(4 * FEAT, PATCHES), hgt_ref[...])
             ws_ref[pl.ds(chip * 2, 2)] = block.astype(BF16).reshape(2, ROWS, 3 * HDIM)
             core_copy(shift, line_of).start()
-    att_ref[...] = dot(values, soft_r).T.astype(BF16)
+
+    share(2)
+    share(1)
+    all_landed("other", oland, 2)
+    for which, sign in enumerate((1, -1)):
+        total = pull_ref[theirs + along(-6 * sign)].astype(F32) + oland[which].astype(F32)
+        pull_ref[theirs + along(-6 * sign)] = total.astype(BF16)
+        back_over(6 * sign).start()
+    for offset in NEAR + (3, -3, 1, -1, 0):
+        back_over(offset).start()
+    share(3)
+    for offset in (8, 7, -7):
+        pass_on(offset, gathered(offset, ()))
+    share(0)
+    for shift in (2, 1, 3):
+        core_sum(shift, 0)
+        core_sum(shift, 1)
+        if shift == 2:
+            place_copy(2, 0).start()
+            place_copy(2, 1).start()
+    place_copy(1, 1).start()
+    place_copy(3, 0).start()
     sums_over.wait_recv()
     spair[...] = spair[...] + sums[...]
     for offset in FAR + NEAR + (1, -1):
         back_sums(offset, spair).start()
-
+    att_ref[...] = dot(values, soft_r).T.astype(BF16)
+    att_copy = pltpu.make_async_copy(att_ref, att_any, local.at[3])
+    att_copy.start()
+
+    def eighth(sign):
+        return (1 - core if sign > 0 else core).astype(F32)
+
+    all_landed("z far", zland, len(FAR))
     for sign in (1, -1):
-        total = pull_ref[theirs + along(-6 * sign)].astype(F32)
-        total = total + landed(back_other, oland, 5 * sign) + landed(back_other, oland, 7 * sign)
-        if sign > 0:
-            back_other(8).wait_recv()
-        mask = (1 - core if sign > 0 else core).astype(F32)
-        total = total + mask * oland[8].astype(F32)
-        pull_ref[theirs + along(-6 * sign)] = total.astype(BF16)
-        back_over(6 * sign).start()
-    for offset in (1, -1, 0):
-        back_over(offset).start()
-    for shift in shifts[:-1]:
-        core_sum(shift, 0)
-        core_sum(shift, 1)
-        place_copy(shift).start()
-
-    def gathered(offset, inputs):
-        total = pull_ref[mine + along(-offset)].astype(F32) + landed(back_over, yland, offset)
-        for at in inputs:
-            total = total + landed(back, zland, at)
-        return total
-
-    def pass_on(offset, total):
-        pull_ref[mine + along(-offset)] = total.astype(BF16)
-        back(offset).start()
-
-    def sums_of(inputs):
-        total = spair[...]
-        for at in inputs:
-            back_sums(at, spair).wait_recv()
-            total = total + sland[at % NZ]
-        return total
-
+        total = gathered(6 * sign, ())
+        for offset in (5 * sign, 7 * sign):
+            total = total + zland[offset % NZ].astype(F32)
+        pass_on(6 * sign, total + eighth(sign) * zland[8].astype(F32))
+    sums_landed(0, len(FAR))
+    for which, sign in enumerate((1, -1)):
+        total = spair[...] + eighth(sign) * sland[8]
+        spart[which] = total + sland[(5 * sign) % NZ] + sland[(7 * sign) % NZ]
+        back_sums(6 * sign, spart.at[which]).start()
     for offset in NEAR:
         pass_on(offset, gathered(offset, ()))
-    for sign in (1, -1):
-        total = gathered(6 * sign, (5 * sign, 7 * sign))
-        if sign > 0:
-            back(8).wait_recv()
-        mask = (1 - core if sign > 0 else core).astype(F32)
-        pass_on(6 * sign, total + mask * zland[8].astype(F32))
-    for which, sign in enumerate((1, -1)):
-        if sign > 0:
-            back_sums(8, spair).wait_recv()
-        mask = (1 - core if sign > 0 else core).astype(F32)
-        spart[which] = sums_of((5 * sign, 7 * sign)) + mask * sland[8]
-        back_sums(6 * sign, spart.at[which]).start()
+    merge(1, 0)
+    merge(3, 1)
     for offset in (1, -1):
         pass_on(offset, gathered(offset, ()))
     core_sum(0, 0)
     core_sum(0, 1)
     for sign in (1, -1):
         pass_on(3 * sign, gathered(3 * sign, (2 * sign, 4 * sign, 6 * sign)))
+    sums_landed(1, 6)
     for which, sign in enumerate((1, -1)):
-        spart[2 + which] = sums_of((2 * sign, 4 * sign, 6 * sign))
+        total = spair[...]
+        for offset in (2 * sign, 4 * sign, 6 * sign):
+            total = total + sland[offset % NZ]
+        spart[2 + which] = total
         back_sums(3 * sign, spart.at[2 + which]).start()
+    for shift in (1, 3):
+        place_copy(shift, 0).wait_recv()
+        place_copy(shift, 1).wait_recv()
     far = cland[0, 1 - line].astype(F32)
-    for shift in (1, 2, 3):
-        place_copy(shift).wait_recv()
-        far = far + xland[shift - 1, 1 - line].astype(F32)
+    for side in (0, 1):
+        far = far + xland[side, 1 - line].astype(F32)
     hstage[...] = far.astype(BF16)
     line_copy = remote(hstage, hland, hsend.at[0], hrecv.at[0], across_line)
     line_copy.start()
     near = cland[0, line].astype(F32)
-    for shift in (1, 2, 3):
-        near = near + xland[shift - 1, line].astype(F32)
+    for side in (0, 1):
+        near = near + xland[side, line].astype(F32)
     wg_ref[...] = near
 
     normed = (g_ref[mp].astype(F32) - average) * inverse
@@ -482,44 +517,42 @@
         [jnp.sum(turned, axis=0, keepdims=True), jnp.zeros((1, 128 - FEAT), F32)], axis=1
     )
 
-    def gain_copy(steps):
-        slot = steps[0] * 8 + steps[1] * 2 + steps[2]
-        return remote(gstage, gland.at[slot], gsend.at[slot], grecv.at[slot], at_dp(*steps))
-
-    for steps in others:
-        gain_copy(steps).start()
-    sum_all = sums_of((1, -1, 3, -3))
+    for i, steps in enumerate(others):
+        remote(gstage, gland.at[i], gsend.at[0], grecv.at[0], at_dp(*steps)).start()
+    sums_landed(2, 4)
+    sum_all = spair[...]
+    for offset in (1, -1, 3, -3):
+        sum_all = sum_all + sland[offset % NZ]
     own_gain = gb_ref[mp].astype(F32)
     scaled = pull * jnp.concatenate([own_gain, own_gain], axis=1)
     ig_ref[...] = (
         inverse * (scaled - sum_all[0] * (1.0 / D) - normed * (sum_all[1] * (1.0 / D)))
     ).astype(BF16)
+    ig_copy = pltpu.make_async_copy(ig_ref, ig_any, local.at[4])
+    ig_copy.start()
     line_copy.wait_recv()
     wg_ref[...] += hland[...].astype(F32)
+    wg_copy = pltpu.make_async_copy(wg_ref, wg_any, local.at[5])
+    wg_copy.start()
+    Both("z far", partner, 0, NMP - 1).wait_send()
+    part = pull_ref.at[pl.ds(0, 15 + 14 + 2)]
+    scatter_copy("z far", part, part, partner).wait_send()
+    part = sland.at[pl.ds(0, NZ - 1)]
+    remote(part, part, ssend.at[0], srecv.at[0], partner).wait_send()
     sums_over.wait_send()
-    for offset in (1, 2, 3, 4, 5, 6, 7, 8, -1, -2, -3, -4, -5, -6, -7):
-        spread(offset).wait_send()
-        back(offset).wait_send()
-        back_sums(offset, spair).wait_send()
-        if offset in FAR:
-            other(offset).wait_send()
-            back_other(offset).wait_send()
-        else:
-            over(offset).wait_send()
-            back_over(offset).wait_send()
-    over(0).wait_send()
-    back_over(0).wait_send()
-    for shift in shifts:
-        core_copy(shift, 0).wait_send()
-        core_copy(shift, 1).wait_send()
-        if shift > 0:
-            place_copy(shift).wait_send()
+    part = ws_ref.at[pl.ds(0, 8)]
+    remote(part, part, csend.at[0], crecv.at[0], mate).wait_send()
+    part = ws_ref.at[pl.ds(0, 6)]
+    remote(part, part, xsend.at[0], xrecv.at[0], mate).wait_send()
     line_copy.wait_send()
+    remote(gland, gland, gsend.at[0], grecv.at[0], mate).wait()
     gain_total = gstage[...]
-    for steps in others:
-        gain_copy(steps).wait()
-        gain_total = gain_total + gland[steps[0] * 8 + steps[1] * 2 + steps[2]]
+    for i in range(len(others)):
+        gain_total = gain_total + gland[i]
     gg_ref[...] = gain_total
+    att_copy.wait()
+    ig_copy.wait()
+    wg_copy.wait()
 
 
 def fused(x, gain, weights, out_grad):
@@ -538,8 +571,16 @@
             pl.BlockSpec(memory_space=pltpu.HBM),
             pl.BlockSpec(memory_space=pltpu.HBM),
         ],
-        out_specs=tuple([pl.BlockSpec(memory_space=VMEM)] * 4),
+        out_specs=(
+            pl.BlockSpec(memory_space=pltpu.HBM),
+            pl.BlockSpec(memory_space=pltpu.HBM),
+            pl.BlockSpec(memory_space=pltpu.HBM),
+            pl.BlockSpec(memory_space=VMEM),
+        ),
         scratch_shapes=[
+            VMEM((PATCHES, HDIM), BF16),
+            VMEM((FEAT, PATCHES), BF16),
+            VMEM((ROWS, 3 * HDIM), F32),
             VMEM((D, 3 * HDIM), BF16),
             VMEM((PATCHES, HDIM), BF16),
             VMEM((NMP, FEAT, PATCHES), BF16),
@@ -554,54 +595,88 @@
             VMEM((2 * CHIPS, ROWS, 3 * HDIM), BF16),
             VMEM((NZ, FEAT, PATCHES), BF16),
             VMEM((NZ, FEAT, PATCHES), BF16),
-            VMEM((NZ, FEAT, PATCHES), BF16),
+            VMEM((2, FEAT, PATCHES), BF16),
             VMEM((2, 1, PATCHES), F32),
             VMEM((2, 1, PATCHES), F32),
             VMEM((NZ, 2, 1, PATCHES), F32),
             VMEM((4, 2, 1, PATCHES), F32),
             VMEM((4, 2, ROWS, 3 * HDIM), BF16),
-            VMEM((3, 2, ROWS, 3 * HDIM), BF16),
+            VMEM((2, ROWS, 3 * HDIM), BF16),
+            VMEM((2, 2, ROWS, 3 * HDIM), BF16),
             VMEM((ROWS, 3 * HDIM), BF16),
             VMEM((ROWS, 3 * HDIM), BF16),
             VMEM((1, 128), F32),
-            VMEM((2 * CHIPS, 1, 128), F32),
-            dma((3,)),
-            dma((2, NZ)),
-            dma((2, NZ)),
-            dma((2, NZ)),
-            dma((2, NZ)),
-            dma((2, NZ)),
-            dma((2, NZ)),
-            dma((NZ,)),
-            dma((NZ,)),
+            VMEM((2 * CHIPS - 1, 1, 128), F32),
+            dma((6,)),
+            dma((2,)),
+            dma((2, len(GATHER_SLOTS))),
+            dma((1,)),
+            dma((len(SCATTER_SLOTS),)),
+            dma((2,)),
+            dma((4,)),
+            dma((1,)),
+            dma((8,)),
+            dma((1,)),
+            dma((6,)),
             dma((1,)),
             dma((1,)),
-            dma((NZ,)),
-            dma((NZ,)),
-            dma((NZ,)),
-            dma((NZ,)),
-            dma((NZ,)),
-            dma((NZ,)),
-            dma((8,)),
-            dma((8,)),
-            dma((3,)),
-            dma((3,)),
             dma((1,)),
             dma((1,)),
-            dma((2 * CHIPS,)),
-            dma((2 * CHIPS,)),
         ],
         compiler_params=pltpu.CompilerParams(
-            collective_id=0, has_side_effects=True, vmem_limit_bytes=28 << 20
+            collective_id=0, has_side_effects=True, vmem_limit_bytes=56 << 20
         ),
     )(x, gain, weights, out_grad)
 
 
+def finish_kernel(
+    att_in, ig_in, wg_in, gg_in, att_ref, ig_ref, wg_ref, gg_ref, att, ig, wg, local
+):
+    loads = [
+        pltpu.make_async_copy(source, held, local.at[i])
+        for i, (source, held) in enumerate(((wg_in, wg), (att_in, att), (ig_in, ig)))
+    ]
+    for load in loads:
+        load.start()
+    stores = [
+        pltpu.make_async_copy(held, target, local.at[3 + i])
+        for i, (held, target) in enumerate(((wg, wg_ref.at[:, 0, :]), (att, att_ref), (ig, ig_ref)))
+    ]
+    gg_ref[...] = gg_in[:, :FEAT]
+    for load, store in zip(loads, stores):
+        load.wait()
+        store.start()
+    for store in stores:
+        store.wait()
+
+
+def finish(attended, input_grad, weight_grad, gain_grad):
+    hbm, vmem = pl.BlockSpec(memory_space=pltpu.HBM), pl.BlockSpec(memory_space=VMEM)
+    return pl.pallas_call(
+        finish_kernel,
+        out_shape=(
+            jax.ShapeDtypeStruct((PATCHES, HDIM), BF16),
+            jax.ShapeDtypeStruct((FEAT, PATCHES), BF16),
+            jax.ShapeDtypeStruct((ROWS, 1, 3 * HDIM), F32),
+            jax.ShapeDtypeStruct((1, FEAT), F32),
+        ),
+        in_specs=[hbm, hbm, hbm, vmem],
+        out_specs=(hbm, hbm, hbm, vmem),
+        scratch_shapes=[
+            VMEM((PATCHES, HDIM), BF16),
+            VMEM((FEAT, PATCHES), BF16),
+            VMEM((ROWS, 3 * HDIM), F32),
+            pltpu.SemaphoreType.DMA((6,)),
+        ],
+        compiler_params=pltpu.CompilerParams(vmem_limit_bytes=56 << 20),
+    )(attended, input_grad, weight_grad, gain_grad)
+
+
 def on_device(tokens, gain, w_qkv, out_grad):
-    attended, input_grad, weight_grad, gain_grad = fused(
-        tokens.T, gain.reshape(1, FEAT), w_qkv[:, 0, :], out_grad
+    attended, input_grad, weight_grad, gain_grad = finish(
+        *fused(tokens.T, gain.reshape(1, FEAT), w_qkv[:, 0, :], out_grad)
     )
-    return attended, input_grad.T, weight_grad[:, None, :], gain_grad[0, :FEAT]
+    return attended, input_grad.T, weight_grad, gain_grad.reshape(FEAT)
 
 
 def solution(mesh):

time: 79.7 us -> 72.8 us (0.913)
  local copies, waits for them, and re-layouts: 6.73 us -> 0 us
    unnamed x11 -> x0, local copies, waits for them, and re-layouts: 6.22 us -> none
    pallas_call x1, Pallas kernels: 72 us -> 69.1 us  [fused(): pl.pallas_call(fused_kernel, out_shape=(jax.ShapeDtypeStruct((PATCHES, HD...]
    pallas_call x0 -> x1, Pallas kernels: none -> 2.87 us  [finish(): pl.pallas_call(finish_kernel, out_shape=(jax.ShapeDtypeStruct((PATCHES, H...]
where the time goes in v4:
time: 72.8 us; the launch traced here: 72.6 us
  Pallas kernels  71.9 us (99%)
    pallas_call x1, Pallas kernels, fused(): pl.pallas_call(fused_kernel, out_shape=(jax.ShapeDtypeStruct((PATCHES, HD...  69.1 us
    pallas_call x1, Pallas kernels, finish(): pl.pallas_call(finish_kernel, out_shape=(jax.ShapeDtypeStruct((PATCHES, H...  2.87 us

profile of v4, /device:TPU:1, one launch (start us, length us, event | category | flops | bytes accessed | tf_op | source)
XLA Modules:
  0.0 72.6 jit_solution(1498865353144614471)
XLA Ops:
  0.6 69.1 %shard_map.75 = (bf16[256,128]{1,0:T(8,128)(2,1)}, bf16[96,256]{1,0:T(8,128)(2,1)}, f32[192,384]{1,0:T(8,128)}, f32[1,128]{1,0:T(1,128)}) custom-call(bf16[96,256]{1,0:T(8,128)(2,1)} %bitcast.6, bf16[1,96]{1,0:T(2,128)(2,1)} %bitcast.7, bf16[3072,384]{1,0:T(8,128)(2,1)} %bitcast.5, bf16[256,128]{1,0:T(8,128)(2,1)} %do_any.1), custom_call_target="tpu_custom_call" | custom-call | tf_op jit(solution)/shard_map/pallas_call | solution.py:560
  69.7 2.9 %shard_map.76 = (bf16[256,128]{1,0:T(8,128)(2,1)}, bf16[96,256]{1,0:T(8,128)(2,1)}, f32[192,1,384]{2,1,0:T(1,128)}, f32[1,96]{1,0:T(1,128)}) custom-call(bf16[256,128]{1,0:T(8,128)(2,1)} %get-tuple-element.12.att_in, bf16[96,256]{1,0:T(8,128)(2,1)} %get-tuple-element.13.ig_in, f32[192,384]{1,0:T(8,128)} %get-tuple-element.14.wg_in, ...), custom_call_target="tpu_custom_call" | custom-call | tf_op jit(solution)/shard_map/pallas_call | solution.py:655

commit v5 on v4

--- a/solution.py
+++ b/solution.py
@@ -70,19 +70,27 @@
 FAR = (5, -5, 7, -7, 8)
 FIVES = (5, -5)
 NEAR = (2, -2, 4, -4)
+HALVES = (0, 1)
 GATHER_SLOTS = (
-    *(("z", offset) for offset in (3, -3, 1, -1, 6, -6) + NEAR),
-    *(("y", offset) for offset in (6, -6)),
+    *(("z", offset, half) for offset in (3, -3, 6, -6) for half in HALVES),
+    *(("z", offset, None) for offset in (1, -1) + NEAR),
+    *(("y", offset, half) for offset in (6, -6) for half in HALVES),
     "z far",
     "y near",
     "other",
 )
 SCATTER_SLOTS = (
-    *(("z", offset) for offset in NEAR + (6, -6, 3, -3, 1, -1)),
-    *(("y", offset) for offset in (8, 7, -7, 6, -6, 3, -3, 1, -1, 0) + NEAR),
-    "z far",
+    *(("z", offset, half) for offset in (6, -6, 3, -3) for half in HALVES),
+    *(("z", offset, None) for offset in NEAR + (1, -1)),
+    *(("y", offset, half) for offset in (8, 7, -7) for half in HALVES),
+    *(("y", offset, None) for offset in (6, -6, 3, -3, 1, -1, 0) + NEAR),
+    *(("z far", half) for half in HALVES),
     "other",
 )
+
+
+def rows_of(half):
+    return slice(None) if half is None else pl.ds(half * (FEAT // 2), FEAT // 2)
 
 
 def fused_kernel(
@@ -184,13 +192,13 @@
     pl.semaphore_wait(barrier, len(peers))
 
     class Both:
-        def __init__(self, key, target, block, count=1):
+        def __init__(self, key, target, block, half=None):
             slot = GATHER_SLOTS.index(key)
-            part = block if count == 1 else pl.ds(block, count)
-            self.copies = [
-                remote(ref.at[part], ref.at[part], bsend.at[i], brecv.at[i, slot], target)
-                for i, ref in enumerate((g_ref, gains))
-            ]
+            part = g_ref.at[block, rows_of(half)]
+            self.copies = [remote(part, part, bsend.at[0], brecv.at[0, slot], target)]
+            if half != 1:
+                part = gains.at[block]
+                self.copies.append(remote(part, part, bsend.at[1], brecv.at[1, slot], target))
 
         def start(self):
             for copy in self.copies:
@@ -204,28 +212,29 @@
             for copy in self.copies:
                 copy.wait_recv()
 
-    def spread(offset):
-        key = "z far" if offset in FAR else ("z", offset)
-        return Both(key, at_z(offset - hub(offset)), mine + along(-hub(offset)))
-
-    def arrived(offset):
-        Both(("z", offset), at_z(1), mine + along(-offset)).wait_recv()
-
-    def over(offset):
-        key = ("y", offset) if abs(offset) == 6 else "y near"
-        return Both(key, partner, mine + along(-offset))
-
-    def over_arrived(offset):
-        Both(("y", offset), partner, theirs + along(-offset)).wait_recv()
-
-    def other(offset):
-        return Both("other", at_z(offset - hub(offset)), theirs + along(-hub(offset)))
+    def spread(offset, half=None):
+        key = "z far" if offset in FAR else ("z", offset, half)
+        return Both(key, at_z(offset - hub(offset)), mine + along(-hub(offset)), half)
+
+    def arrived(offset, half=None):
+        Both(("z", offset, half), at_z(1), mine + along(-offset), half).wait_recv()
+
+    def over(offset, half=None):
+        key = ("y", offset, half) if abs(offset) == 6 else "y near"
+        return Both(key, partner, mine + along(-offset), half)
+
+    def over_arrived(offset, half=None):
+        Both(("y", offset, half), partner, theirs + along(-offset), half).wait_recv()
+
+    def other(offset, half=None):
+        return Both("other", at_z(offset - hub(offset)), theirs + along(-hub(offset)), half)
 
     def all_arrived(key, count):
-        Both(key, partner, 0, count).wait_recv()
-
-    for offset in (3, -3):
-        spread(offset).start()
+        Both(key, partner, pl.ds(0, count)).wait_recv()
+
+    for half in HALVES:
+        for offset in (3, -3):
+            spread(offset, half).start()
     over(0).start()
     for offset in (1, -1):
         spread(offset).start()
@@ -234,28 +243,33 @@
         wt_ref[:, part * 256 : (part + 1) * 256] = w_ref[part * 256 : (part + 1) * 256, :].T
     do_copy.wait()
     cotangent = do_ref[...].T
+    for half in HALVES:
+        for sign in (1, -1):
+            arrived(3 * sign, half)
+            spread(6 * sign, half).start()
     for sign in (1, -1):
-        arrived(3 * sign)
-        for offset in (6 * sign, 4 * sign, 2 * sign):
-            spread(offset).start()
+        spread(4 * sign).start()
+        spread(2 * sign).start()
         over(3 * sign).start()
     for offset in (1, -1):
         arrived(offset)
         over(offset).start()
-    for sign in (1, -1):
-        arrived(6 * sign)
-        over(6 * sign).start()
-        for offset in (5 * sign, 7 * sign):
-            spread(offset).start()
-    spread(8).start()
+    for half in HALVES:
+        for sign in (1, -1):
+            arrived(6 * sign, half)
+            over(6 * sign, half).start()
+            spread(5 * sign, half).start()
+            spread(7 * sign, half).start()
+        spread(8, half).start()
     for offset in NEAR:
         arrived(offset)
         over(offset).start()
-    for sign in (1, -1):
-        over_arrived(6 * sign)
-        for offset in (5 * sign, 7 * sign):
-            other(offset).start()
-    other(8).start()
+    for half in HALVES:
+        for sign in (1, -1):
+            over_arrived(6 * sign, half)
+            other(5 * sign, half).start()
+            other(7 * sign, half).start()
+        other(8, half).start()
     all_arrived("z far", len(FAR))
 
     shift_row = jnp.sum(g_ref[mp].astype(F32), axis=0, keepdims=True) * (1.0 / FEAT)
@@ -281,9 +295,12 @@
     gain_columns(mine)
     gain_weights = gain_product(mine)
     all_arrived("y near", 9)
+    for offset in (0, 1, -1, 2, -2, 3, -3, 4, -4, 6, -6):
+        totals = add_block(theirs + along(-offset), totals)
     all_arrived("other", len(FAR))
     gain_columns(theirs)
-    totals = lax.fori_loop(theirs, theirs + NZ, add_block, totals)
+    for offset in FAR:
+        totals = add_block(theirs + along(-offset), totals)
     first = jnp.sum(totals[0], axis=0, keepdims=True) * (1.0 / D)
     second = jnp.sum(totals[1], axis=0, keepdims=True) * (1.0 / D)
     average = shift_row + first
@@ -331,21 +348,22 @@
     def scatter_copy(key, src, dst, target):
         return remote(src, dst, rsend.at[0], rrecv.at[SCATTER_SLOTS.index(key)], target)
 
-    def back_over(offset):
-        src = pull_ref.at[theirs + along(-offset)]
-        return scatter_copy(("y", offset), src, yland.at[offset % NZ], partner)
+    def back_over(offset, half=None):
+        rows = rows_of(half)
+        src = pull_ref.at[theirs + along(-offset), rows]
+        return scatter_copy(("y", offset, half), src, yland.at[offset % NZ, rows], partner)
 
     def back_other(offset):
         src = pull_ref.at[theirs + along(-offset)]
         return scatter_copy("other", src, oland.at[FIVES.index(offset)], at_z(hub(offset) - offset))
 
-    def back(offset):
-        key = "z far" if offset in FAR else ("z", offset)
-        src = pull_ref.at[mine + along(-offset)]
-        return scatter_copy(key, src, zland.at[offset % NZ], at_z(hub(offset) - offset))
-
-    def all_landed(key, land, count):
-        part = land.at[pl.ds(0, count)]
+    def back(offset, half=None):
+        rows = rows_of(half)
+        key = ("z far", half) if offset in FAR else ("z", offset, half)
+        src = pull_ref.at[mine + along(-offset), rows]
+        return scatter_copy(key, src, zland.at[offset % NZ, rows], at_z(hub(offset) - offset))
+
+    def all_landed(key, part):
         scatter_copy(key, part, part, partner).wait_recv()
 
     def back_sums(offset, src):
@@ -362,28 +380,34 @@
         part = sland.at[pl.ds(0, count)]
         remote(part, part, ssend.at[0], srecv.at[stage], partner).wait_recv()
 
-    def landed(copy, land, offset):
-        copy(offset).wait_recv()
-        return land[offset % NZ].astype(F32)
-
-    def gathered(offset, inputs):
-        total = pull_ref[mine + along(-offset)].astype(F32) + landed(back_over, yland, offset)
-        for at in inputs:
-            total = total + landed(back, zland, at)
+    def part_of(ref, block, half):
+        return ref[block, rows_of(half)].astype(F32)
+
+    def gathered(offset, half, over_half, inputs):
+        total = part_of(pull_ref, mine + along(-offset), half)
+        if over_half == half:
+            back_over(offset, half).wait_recv()
+        total = total + part_of(yland, offset % NZ, half)
+        for at, at_half in inputs:
+            if at_half == half:
+                back(at, half).wait_recv()
+            total = total + part_of(zland, at % NZ, half)
         return total
 
-    def pass_on(offset, total):
-        pull_ref[mine + along(-offset)] = total.astype(BF16)
-        back(offset).start()
+    def pass_on(offset, half, total):
+        pull_ref[mine + along(-offset), rows_of(half)] = total.astype(BF16)
+        back(offset, half).start()
 
     pull_rows(theirs)
     for offset in FIVES:
         back_other(offset).start()
-    for offset in (8, 7, -7):
-        back_over(offset).start()
+    for half in HALVES:
+        for offset in (8, 7, -7):
+            back_over(offset, half).start()
     pull_rows(mine)
-    for offset in FIVES:
-        back(offset).start()
+    for half in HALVES:
+        for offset in FIVES:
+            back(offset, half).start()
     gain_weights = gain_weights + gain_product(theirs)
     hg_wide = hg.astype(F32)
     factor = jnp.concatenate([gain_weights, gain_weights], axis=1)
@@ -437,7 +461,7 @@
 
     share(2)
     share(1)
-    all_landed("other", oland, 2)
+    all_landed("other", oland)
     for which, sign in enumerate((1, -1)):
         total = pull_ref[theirs + along(-6 * sign)].astype(F32) + oland[which].astype(F32)
         pull_ref[theirs + along(-6 * sign)] = total.astype(BF16)
@@ -445,8 +469,9 @@
     for offset in NEAR + (3, -3, 1, -1, 0):
         back_over(offset).start()
     share(3)
-    for offset in (8, 7, -7):
-        pass_on(offset, gathered(offset, ()))
+    for half in HALVES:
+        for offset in (8, 7, -7):
+            pass_on(offset, half, gathered(offset, half, half, ()))
     share(0)
     for shift in (2, 1, 3):
         core_sum(shift, 0)
@@ -467,27 +492,34 @@
     def eighth(sign):
         return (1 - core if sign > 0 else core).astype(F32)
 
-    all_landed("z far", zland, len(FAR))
-    for sign in (1, -1):
-        total = gathered(6 * sign, ())
-        for offset in (5 * sign, 7 * sign):
-            total = total + zland[offset % NZ].astype(F32)
-        pass_on(6 * sign, total + eighth(sign) * zland[8].astype(F32))
+    back_over(6).wait_recv()
+    back_over(-6).wait_recv()
+    for half in HALVES:
+        all_landed(("z far", half), zland.at[pl.ds(0, len(FAR)), rows_of(half)])
+        for sign in (1, -1):
+            total = gathered(6 * sign, half, -1, ((5 * sign, -1), (7 * sign, -1)))
+            pass_on(6 * sign, half, total + eighth(sign) * part_of(zland, 8, half))
     sums_landed(0, len(FAR))
     for which, sign in enumerate((1, -1)):
         total = spair[...] + eighth(sign) * sland[8]
         spart[which] = total + sland[(5 * sign) % NZ] + sland[(7 * sign) % NZ]
         back_sums(6 * sign, spart.at[which]).start()
     for offset in NEAR:
-        pass_on(offset, gathered(offset, ()))
+        pass_on(offset, None, gathered(offset, None, None, ()))
     merge(1, 0)
     merge(3, 1)
     for offset in (1, -1):
-        pass_on(offset, gathered(offset, ()))
+        pass_on(offset, None, gathered(offset, None, None, ()))
     core_sum(0, 0)
     core_sum(0, 1)
     for sign in (1, -1):
-        pass_on(3 * sign, gathered(3 * sign, (2 * sign, 4 * sign, 6 * sign)))
+        back_over(3 * sign).wait_recv()
+        back(2 * sign).wait_recv()
+        back(4 * sign).wait_recv()
+    for half in HALVES:
+        for sign in (1, -1):
+            inputs = ((2 * sign, -1), (4 * sign, -1), (6 * sign, half))
+            pass_on(3 * sign, half, gathered(3 * sign, half, -1, inputs))
     sums_landed(1, 6)
     for which, sign in enumerate((1, -1)):
         total = spair[...]
@@ -510,7 +542,11 @@
     wg_ref[...] = near
 
     normed = (g_ref[mp].astype(F32) - average) * inverse
-    pull = gathered(0, (1, -1, 3, -3))
+    pull = gathered(0, None, None, ((1, None), (-1, None)))
+    for offset in (3, -3):
+        for half in HALVES:
+            back(offset, half).wait_recv()
+        pull = pull + part_of(zland, offset % NZ, None)
     product = pull * normed
     turned = (product[:, :128] + product[:, 128:]).T
     gstage[...] = jnp.concatenate(
@@ -534,9 +570,9 @@
     wg_ref[...] += hland[...].astype(F32)
     wg_copy = pltpu.make_async_copy(wg_ref, wg_any, local.at[5])
     wg_copy.start()
-    Both("z far", partner, 0, NMP - 1).wait_send()
+    Both("z far", partner, pl.ds(0, NMP - 1)).wait_send()
     part = pull_ref.at[pl.ds(0, 15 + 14 + 2)]
-    scatter_copy("z far", part, part, partner).wait_send()
+    scatter_copy("other", part, part, partner).wait_send()
     part = sland.at[pl.ds(0, NZ - 1)]
     remote(part, part, ssend.at[0], srecv.at[0], partner).wait_send()
     sums_over.wait_send()
@@ -630,28 +666,33 @@
 
 
 def finish_kernel(
-    att_in, ig_in, wg_in, gg_in, att_ref, ig_ref, wg_ref, gg_ref, att, ig, wg, local
+    att_in, ig_in, wg_in, gg_in, att_ref, ig_ref, wg_ref, gg_ref, att, ig, wg, gg, ggs, local
 ):
+    moves = (
+        (wg_in, wg, wg, wg_ref.at[:, 0, :]),
+        (att_in, att, att, att_ref),
+        (gg_in, gg, ggs, gg_ref),
+        (ig_in, ig, ig, ig_ref),
+    )
     loads = [
-        pltpu.make_async_copy(source, held, local.at[i])
-        for i, (source, held) in enumerate(((wg_in, wg), (att_in, att), (ig_in, ig)))
+        pltpu.make_async_copy(move[0], move[1], local.at[0, i]) for i, move in enumerate(moves)
+    ]
+    stores = [
+        pltpu.make_async_copy(move[2], move[3], local.at[1, i]) for i, move in enumerate(moves)
     ]
     for load in loads:
         load.start()
-    stores = [
-        pltpu.make_async_copy(held, target, local.at[3 + i])
-        for i, (held, target) in enumerate(((wg, wg_ref.at[:, 0, :]), (att, att_ref), (ig, ig_ref)))
-    ]
-    gg_ref[...] = gg_in[:, :FEAT]
-    for load, store in zip(loads, stores):
-        load.wait()
-        store.start()
+    for i in range(4):
+        loads[i].wait()
+        if i == 2:
+            ggs[...] = gg[:, :FEAT]
+        stores[i].start()
     for store in stores:
         store.wait()
 
 
 def finish(attended, input_grad, weight_grad, gain_grad):
-    hbm, vmem = pl.BlockSpec(memory_space=pltpu.HBM), pl.BlockSpec(memory_space=VMEM)
+    hbm = pl.BlockSpec(memory_space=pltpu.HBM)
     return pl.pallas_call(
         finish_kernel,
         out_shape=(
@@ -660,13 +701,15 @@
             jax.ShapeDtypeStruct((ROWS, 1, 3 * HDIM), F32),
             jax.ShapeDtypeStruct((1, FEAT), F32),
         ),
-        in_specs=[hbm, hbm, hbm, vmem],
-        out_specs=(hbm, hbm, hbm, vmem),
+        in_specs=[hbm] * 4,
+        out_specs=(hbm,) * 4,
         scratch_shapes=[
             VMEM((PATCHES, HDIM), BF16),
             VMEM((FEAT, PATCHES), BF16),
             VMEM((ROWS, 3 * HDIM), F32),
-            pltpu.SemaphoreType.DMA((6,)),
+            VMEM((1, 128), F32),
+            VMEM((1, FEAT), F32),
+            pltpu.SemaphoreType.DMA((2, 4)),
         ],
         compiler_params=pltpu.CompilerParams(vmem_limit_bytes=56 << 20),
     )(attended, input_grad, weight_grad, gain_grad)

time: 72.8 us -> 69.8 us (0.959)
  Pallas kernels: 71.9 us -> 69 us
    pallas_call x1, Pallas kernels: 69.1 us -> 67.2 us  [fused(): pl.pallas_call(fused_kernel, out_shape=(jax.ShapeDtypeStruct((PATCHES, HD...]
    pallas_call x1, Pallas kernels: 2.87 us -> 1.77 us  [finish(): pl.pallas_call(finish_kernel, out_shape=(jax.ShapeDtypeStruct((PATCHES, H...]
where the time goes in v5:
time: 69.8 us; the launch traced here: 69.6 us
  Pallas kernels  69 us (99%)
    pallas_call x1, Pallas kernels, fused(): pl.pallas_call(fused_kernel, out_shape=(jax.ShapeDtypeStruct((PATCHES, HD...  67.2 us
    pallas_call x1, Pallas kernels, finish(): pl.pallas_call(finish_kernel, out_shape=(jax.ShapeDtypeStruct((PATCHES, H...  1.77 us

profile of v5, /device:TPU:1, one launch (start us, length us, event | category | flops | bytes accessed | tf_op | source)
XLA Modules:
  0.0 69.6 jit_solution(10722798343392668114)
XLA Ops:
  0.6 67.2 %shard_map.75 = (bf16[256,128]{1,0:T(8,128)(2,1)}, bf16[96,256]{1,0:T(8,128)(2,1)}, f32[192,384]{1,0:T(8,128)}, f32[1,128]{1,0:T(1,128)}) custom-call(bf16[96,256]{1,0:T(8,128)(2,1)} %bitcast.6, bf16[1,96]{1,0:T(2,128)(2,1)} %bitcast.7, bf16[3072,384]{1,0:T(8,128)(2,1)} %bitcast.5, bf16[256,128]{1,0:T(8,128)(2,1)} %do_any.1), custom_call_target="tpu_custom_call" | custom-call | tf_op jit(solution)/shard_map/pallas_call | solution.py:596
  67.8 1.8 %shard_map.76 = (bf16[256,128]{1,0:T(8,128)(2,1)}, bf16[96,256]{1,0:T(8,128)(2,1)}, f32[192,1,384]{2,1,0:T(1,128)}, f32[1,96]{1,0:T(1,128)}) custom-call(bf16[256,128]{1,0:T(8,128)(2,1)} %get-tuple-element.12.att_in, bf16[96,256]{1,0:T(8,128)(2,1)} %get-tuple-element.13.ig_in, f32[192,384]{1,0:T(8,128)} %get-tuple-element.14.wg_in, ...), custom_call_target="tpu_custom_call" | custom-call | tf_op jit(solution)/shard_map/pallas_call | solution.py:696

commit v6 on v5

--- a/solution.py
+++ b/solution.py
@@ -81,11 +81,13 @@
 )
 SCATTER_SLOTS = (
     *(("z", offset, half) for offset in (6, -6, 3, -3) for half in HALVES),
-    *(("z", offset, None) for offset in NEAR + (1, -1)),
-    *(("y", offset, half) for offset in (8, 7, -7) for half in HALVES),
-    *(("y", offset, None) for offset in (6, -6, 3, -3, 1, -1, 0) + NEAR),
+    *(("z", offset, None) for offset in (1, -1)),
+    *(("y", offset, half) for offset in (8, 7, -7, 6, -6) for half in HALVES),
+    *(("y", offset, None) for offset in (3, -3, 1, -1, 0)),
     *(("z far", half) for half in HALVES),
+    "z near",
     "other",
+    "other near",
 )
 
 
@@ -278,12 +280,12 @@
         moved = g_ref[block].astype(F32) - shift_row
         return totals[0] + folded(moved), totals[1] + folded(moved * moved)
 
-    def gain_columns(start):
-        for i in range(NZ):
-            rows_ref[i : i + 1, :] = gains[start + i]
+    def gain_columns(blocks):
+        for i, block in enumerate(blocks):
+            rows_ref[i : i + 1, :] = gains[block]
         turned = rows_ref[...].T
-        for i in range(NZ):
-            gb_ref[start + i] = jnp.broadcast_to(turned[:FEAT, i : i + 1], (FEAT, 128)).astype(BF16)
+        for i, block in enumerate(blocks):
+            gb_ref[block] = jnp.broadcast_to(turned[:FEAT, i : i + 1], (FEAT, 128)).astype(BF16)
 
     def gain_product(start):
         half = NZ * FEAT
@@ -292,15 +294,18 @@
 
     zero = jnp.zeros((8, PATCHES), F32)
     totals = lax.fori_loop(mine, mine + NZ, add_block, (zero, zero))
-    gain_columns(mine)
+    gain_columns([mine + i for i in range(NZ)])
     gain_weights = gain_product(mine)
     all_arrived("y near", 9)
-    for offset in (0, 1, -1, 2, -2, 3, -3, 4, -4, 6, -6):
-        totals = add_block(theirs + along(-offset), totals)
+    over_blocks = [theirs + along(-offset) for offset in (0, 1, -1, 3, -3, 6, -6) + NEAR]
+    far_blocks = [theirs + along(-offset) for offset in FAR]
+    for block in over_blocks:
+        totals = add_block(block, totals)
+    gain_columns(over_blocks)
     all_arrived("other", len(FAR))
-    gain_columns(theirs)
-    for offset in FAR:
-        totals = add_block(theirs + along(-offset), totals)
+    for block in far_blocks:
+        totals = add_block(block, totals)
+    gain_columns(far_blocks)
     first = jnp.sum(totals[0], axis=0, keepdims=True) * (1.0 / D)
     second = jnp.sum(totals[1], axis=0, keepdims=True) * (1.0 / D)
     average = shift_row + first
@@ -313,7 +318,7 @@
         nt_ref[block] = (normed * factor).astype(BF16)
         return carry
 
-    lax.fori_loop(0, NMP, normalize, 0)
+    lax.fori_loop(0, NMP, normalize, 0, unroll=4)
 
     wide = dot(wt_ref[...], nt_ref[...].reshape(D, PATCHES))
     projected = wide.astype(BF16)
@@ -354,12 +359,15 @@
         return scatter_copy(("y", offset, half), src, yland.at[offset % NZ, rows], partner)
 
     def back_other(offset):
+        key = "other" if offset in FIVES else "other near"
         src = pull_ref.at[theirs + along(-offset)]
-        return scatter_copy("other", src, oland.at[FIVES.index(offset)], at_z(hub(offset) - offset))
+        land = oland.at[(FIVES + NEAR).index(offset)]
+        return scatter_copy(key, src, land, at_z(hub(offset) - offset))
 
     def back(offset, half=None):
         rows = rows_of(half)
         key = ("z far", half) if offset in FAR else ("z", offset, half)
+        key = "z near" if offset in NEAR else key
         src = pull_ref.at[mine + along(-offset), rows]
         return scatter_copy(key, src, zland.at[offset % NZ, rows], at_z(hub(offset) - offset))
 
@@ -398,24 +406,6 @@
         pull_ref[mine + along(-offset), rows_of(half)] = total.astype(BF16)
         back(offset, half).start()
 
-    pull_rows(theirs)
-    for offset in FIVES:
-        back_other(offset).start()
-    for half in HALVES:
-        for offset in (8, 7, -7):
-            back_over(offset, half).start()
-    pull_rows(mine)
-    for half in HALVES:
-        for offset in FIVES:
-            back(offset, half).start()
-    gain_weights = gain_weights + gain_product(theirs)
-    hg_wide = hg.astype(F32)
-    factor = jnp.concatenate([gain_weights, gain_weights], axis=1)
-    sums[0] = jnp.sum(hg_wide * factor, axis=0, keepdims=True)
-    sums[1] = jnp.sum(hg_wide * wide, axis=0, keepdims=True)
-    sums_over = remote(sums, spair, ssend.at[1], srecv.at[3], partner)
-    sums_over.start()
-
     def core_copy(shift, line_of):
         chip = line_of * 4 + place_at(shift)
         slot = shift * 2 + line_of
@@ -452,6 +442,8 @@
 
     hgt_ref[...] = hg.T
 
+    shifts = (2, 1, 3, 0)
+
     def share(shift):
         for line_of in (0, 1):
             chip = line_of * 4 + place_at(shift)
@@ -459,32 +451,74 @@
             ws_ref[pl.ds(chip * 2, 2)] = block.astype(BF16).reshape(2, ROWS, 3 * HDIM)
             core_copy(shift, line_of).start()
 
-    share(2)
-    share(1)
-    all_landed("other", oland)
+    @pl.when(core == 1)
+    def _():
+        for shift in shifts:
+            share(shift)
+
+    pull_rows(theirs)
+    for offset in FIVES:
+        back_other(offset).start()
+    for half in HALVES:
+        for offset in (8, 7, -7):
+            back_over(offset, half).start()
+    for offset in NEAR:
+        back_other(offset).start()
+    pull_rows(mine)
+    for half in HALVES:
+        for offset in FIVES:
+            back(offset, half).start()
+    gain_weights = gain_weights + gain_product(theirs)
+    hg_wide = hg.astype(F32)
+    factor = jnp.concatenate([gain_weights, gain_weights], axis=1)
+    sums[0] = jnp.sum(hg_wide * factor, axis=0, keepdims=True)
+    sums[1] = jnp.sum(hg_wide * wide, axis=0, keepdims=True)
+    sums_over = remote(sums, spair, ssend.at[1], srecv.at[3], partner)
+    sums_over.start()
+
+    @pl.when(core == 0)
+    def _():
+        share(2)
+        share(1)
+
+    all_landed("other", oland.at[pl.ds(0, 2)])
     for which, sign in enumerate((1, -1)):
         total = pull_ref[theirs + along(-6 * sign)].astype(F32) + oland[which].astype(F32)
         pull_ref[theirs + along(-6 * sign)] = total.astype(BF16)
-        back_over(6 * sign).start()
-    for offset in NEAR + (3, -3, 1, -1, 0):
-        back_over(offset).start()
-    share(3)
+    for half in HALVES:
+        for sign in (1, -1):
+            back_over(6 * sign, half).start()
+    for line_of in (0, 1):
+        core_sum(2, line_of)
+        place_copy(2, line_of).start()
     for half in HALVES:
         for offset in (8, 7, -7):
             pass_on(offset, half, gathered(offset, half, half, ()))
-    share(0)
-    for shift in (2, 1, 3):
-        core_sum(shift, 0)
-        core_sum(shift, 1)
-        if shift == 2:
-            place_copy(2, 0).start()
-            place_copy(2, 1).start()
-    place_copy(1, 1).start()
-    place_copy(3, 0).start()
     sums_over.wait_recv()
     spair[...] = spair[...] + sums[...]
     for offset in FAR + NEAR + (1, -1):
         back_sums(offset, spair).start()
+    all_landed("other near", oland.at[pl.ds(0, 4)])
+    for which, sign in enumerate((1, -1)):
+        total = pull_ref[theirs + along(-3 * sign)].astype(F32)
+        total = total + oland[2 + which].astype(F32) + oland[4 + which].astype(F32)
+        pull_ref[theirs + along(-3 * sign)] = total.astype(BF16)
+        back_over(3 * sign).start()
+    for offset in (1, -1, 0):
+        back_over(offset).start()
+    for offset in NEAR:
+        back(offset).start()
+
+    @pl.when(core == 0)
+    def _():
+        share(3)
+        share(0)
+
+    for shift in (1, 3):
+        core_sum(shift, 0)
+        core_sum(shift, 1)
+    place_copy(1, 1).start()
+    place_copy(3, 0).start()
     att_ref[...] = dot(values, soft_r).T.astype(BF16)
     att_copy = pltpu.make_async_copy(att_ref, att_any, local.at[3])
     att_copy.start()
@@ -492,9 +526,9 @@
     def eighth(sign):
         return (1 - core if sign > 0 else core).astype(F32)
 
-    back_over(6).wait_recv()
-    back_over(-6).wait_recv()
-    for half in HALVES:
+    for half in HALVES:
+        back_over(6, half).wait_recv()
+        back_over(-6, half).wait_recv()
         all_landed(("z far", half), zland.at[pl.ds(0, len(FAR)), rows_of(half)])
         for sign in (1, -1):
             total = gathered(6 * sign, half, -1, ((5 * sign, -1), (7 * sign, -1)))
@@ -504,18 +538,13 @@
         total = spair[...] + eighth(sign) * sland[8]
         spart[which] = total + sland[(5 * sign) % NZ] + sland[(7 * sign) % NZ]
         back_sums(6 * sign, spart.at[which]).start()
-    for offset in NEAR:
-        pass_on(offset, None, gathered(offset, None, None, ()))
     merge(1, 0)
     merge(3, 1)
-    for offset in (1, -1):
-        pass_on(offset, None, gathered(offset, None, None, ()))
     core_sum(0, 0)
     core_sum(0, 1)
     for sign in (1, -1):
         back_over(3 * sign).wait_recv()
-        back(2 * sign).wait_recv()
-        back(4 * sign).wait_recv()
+    all_landed("z near", zland.at[pl.ds(0, len(NEAR))])
     for half in HALVES:
         for sign in (1, -1):
             inputs = ((2 * sign, -1), (4 * sign, -1), (6 * sign, half))
@@ -527,6 +556,8 @@
             total = total + sland[offset % NZ]
         spart[2 + which] = total
         back_sums(3 * sign, spart.at[2 + which]).start()
+    for offset in (1, -1):
+        pass_on(offset, None, gathered(offset, None, None, ()))
     for shift in (1, 3):
         place_copy(shift, 0).wait_recv()
         place_copy(shift, 1).wait_recv()
@@ -571,7 +602,7 @@
     wg_copy = pltpu.make_async_copy(wg_ref, wg_any, local.at[5])
     wg_copy.start()
     Both("z far", partner, pl.ds(0, NMP - 1)).wait_send()
-    part = pull_ref.at[pl.ds(0, 15 + 14 + 2)]
+    part = pull_ref.at[pl.ds(0, 15 + 10 + 6)]
     scatter_copy("other", part, part, partner).wait_send()
     part = sland.at[pl.ds(0, NZ - 1)]
     remote(part, part, ssend.at[0], srecv.at[0], partner).wait_send()
@@ -631,7 +662,7 @@
             VMEM((2 * CHIPS, ROWS, 3 * HDIM), BF16),
             VMEM((NZ, FEAT, PATCHES), BF16),
             VMEM((NZ, FEAT, PATCHES), BF16),
-            VMEM((2, FEAT, PATCHES), BF16),
+            VMEM((6, FEAT, PATCHES), BF16),
             VMEM((2, 1, PATCHES), F32),
             VMEM((2, 1, PATCHES), F32),
             VMEM((NZ, 2, 1, PATCHES), F32),

time: 69.8 us -> 66.7 us (0.956)
  Pallas kernels: 69 us -> 65.9 us
    pallas_call x1, Pallas kernels: 67.2 us -> 64.1 us  [fused(): pl.pallas_call(fused_kernel, out_shape=(jax.ShapeDtypeStruct((PATCHES, HD...]
where the time goes in v6:
time: 66.7 us; the launch traced here: 66.5 us
  Pallas kernels  65.9 us (99%)
    pallas_call x1, Pallas kernels, fused(): pl.pallas_call(fused_kernel, out_shape=(jax.ShapeDtypeStruct((PATCHES, HD...  64.1 us
    pallas_call x1, Pallas kernels, finish(): pl.pallas_call(finish_kernel, out_shape=(jax.ShapeDtypeStruct((PATCHES, H...  1.77 us

profile of v6, /device:TPU:1, one launch (start us, length us, event | category | flops | bytes accessed | tf_op | source)
XLA Modules:
  0.0 66.5 jit_solution(6970041705898780229)
XLA Ops:
  0.6 64.1 %shard_map.75 = (bf16[256,128]{1,0:T(8,128)(2,1)}, bf16[96,256]{1,0:T(8,128)(2,1)}, f32[192,384]{1,0:T(8,128)}, f32[1,128]{1,0:T(1,128)}) custom-call(bf16[96,256]{1,0:T(8,128)(2,1)} %bitcast.6, bf16[1,96]{1,0:T(2,128)(2,1)} %bitcast.7, bf16[3072,384]{1,0:T(8,128)(2,1)} %bitcast.5, bf16[256,128]{1,0:T(8,128)(2,1)} %do_any.1), custom_call_target="tpu_custom_call" | custom-call | tf_op jit(solution)/shard_map/pallas_call | solution.py:627
  64.8 1.8 %shard_map.76 = (bf16[256,128]{1,0:T(8,128)(2,1)}, bf16[96,256]{1,0:T(8,128)(2,1)}, f32[192,1,384]{2,1,0:T(1,128)}, f32[1,96]{1,0:T(1,128)}) custom-call(bf16[256,128]{1,0:T(8,128)(2,1)} %get-tuple-element.12.att_in, bf16[96,256]{1,0:T(8,128)(2,1)} %get-tuple-element.13.ig_in, f32[192,384]{1,0:T(8,128)} %get-tuple-element.14.wg_in, ...), custom_call_target="tpu_custom_call" | custom-call | tf_op jit(solution)/shard_map/pallas_call | solution.py:727

commit v7 on v6

--- a/solution.py
+++ b/solution.py
@@ -97,7 +97,7 @@
 
 def fused_kernel(
     x_any,
-    gain_ref,
+    gain_any,
     w_any,
     do_any,
     att_any,
@@ -108,6 +108,7 @@
     ig_ref,
     wg_ref,
     w_ref,
+    gain_ref,
     do_ref,
     g_ref,
     gains,
@@ -180,6 +181,8 @@
     w_copy = pltpu.make_async_copy(w_any, w_ref, local.at[1])
     do_copy = pltpu.make_async_copy(do_any, do_ref, local.at[2])
     own_copy.start()
+    gain_copy = pltpu.make_async_copy(gain_any, gain_ref, local.at[6])
+    gain_copy.start()
     barrier = pltpu.get_barrier_semaphore()
     peers = [at_z(offset) for offset in (3, -3, 2, -2, 1, -1)] + [partner]
     peers += [at_dp(*steps) for steps in others]
@@ -187,6 +190,7 @@
         pl.semaphore_signal(barrier, inc=1, device_id=peer, device_id_type=MESH)
     w_copy.start()
     do_copy.start()
+    gain_copy.wait()
     gains[mp] = jnp.concatenate(
         [gain_ref[...].astype(F32), jnp.zeros((1, 128 - FEAT), F32)], axis=1
     )
@@ -260,18 +264,20 @@
         for sign in (1, -1):
             arrived(6 * sign, half)
             over(6 * sign, half).start()
+        spread(8, half).start()
+        for sign in (1, -1):
             spread(5 * sign, half).start()
             spread(7 * sign, half).start()
-        spread(8, half).start()
     for offset in NEAR:
         arrived(offset)
         over(offset).start()
     for half in HALVES:
         for sign in (1, -1):
             over_arrived(6 * sign, half)
+        other(8, half).start()
+        for sign in (1, -1):
             other(5 * sign, half).start()
             other(7 * sign, half).start()
-        other(8, half).start()
     all_arrived("z far", len(FAR))
 
     shift_row = jnp.sum(g_ref[mp].astype(F32), axis=0, keepdims=True) * (1.0 / FEAT)
@@ -311,16 +317,16 @@
     average = shift_row + first
     inverse = lax.rsqrt(second - first * first + EPS)
 
-    def normalize(block, carry):
-        factor = gb_ref[block].astype(F32)
-        factor = jnp.concatenate([factor, factor], axis=1)
-        normed = (g_ref[block].astype(F32) - average) * inverse
-        nt_ref[block] = (normed * factor).astype(BF16)
-        return carry
-
-    lax.fori_loop(0, NMP, normalize, 0, unroll=4)
-
-    wide = dot(wt_ref[...], nt_ref[...].reshape(D, PATCHES))
+    wide = None
+    for first_block in range(0, NMP, 8):
+        for block in range(first_block, first_block + 8):
+            factor = gb_ref[block].astype(F32)
+            factor = jnp.concatenate([factor, factor], axis=1)
+            normed = (g_ref[block].astype(F32) - average) * inverse
+            nt_ref[block] = (normed * factor).astype(BF16)
+        rows = nt_ref[first_block : first_block + 8].reshape(8 * FEAT, PATCHES)
+        columns = wt_ref[:, first_block * FEAT : (first_block + 8) * FEAT]
+        wide = dot(columns, rows) if wide is None else wide + dot(columns, rows)
     projected = wide.astype(BF16)
     query, query_inverse = unit_columns(projected[:HDIM].astype(F32))
     keys, keys_inverse = unit_columns(projected[HDIM : 2 * HDIM].astype(F32))
@@ -451,6 +457,18 @@
             ws_ref[pl.ds(chip * 2, 2)] = block.astype(BF16).reshape(2, ROWS, 3 * HDIM)
             core_copy(shift, line_of).start()
 
+    def next_places():
+        for shift in (1, 3):
+            core_sum(shift, 0)
+            core_sum(shift, 1)
+        place_copy(1, 1).start()
+        place_copy(3, 0).start()
+
+    def first_place():
+        for line_of in (0, 1):
+            core_sum(2, line_of)
+            place_copy(2, line_of).start()
+
     @pl.when(core == 1)
     def _():
         for shift in shifts:
@@ -468,6 +486,11 @@
     for half in HALVES:
         for offset in FIVES:
             back(offset, half).start()
+    @pl.when(core == 0)
+    def _():
+        share(2)
+        share(1)
+
     gain_weights = gain_weights + gain_product(theirs)
     hg_wide = hg.astype(F32)
     factor = jnp.concatenate([gain_weights, gain_weights], axis=1)
@@ -478,8 +501,8 @@
 
     @pl.when(core == 0)
     def _():
-        share(2)
-        share(1)
+        first_place()
+        share(3)
 
     all_landed("other", oland.at[pl.ds(0, 2)])
     for which, sign in enumerate((1, -1)):
@@ -488,9 +511,8 @@
     for half in HALVES:
         for sign in (1, -1):
             back_over(6 * sign, half).start()
-    for line_of in (0, 1):
-        core_sum(2, line_of)
-        place_copy(2, line_of).start()
+    pl.when(core == 0)(next_places)
+    pl.when(core == 1)(first_place)
     for half in HALVES:
         for offset in (8, 7, -7):
             pass_on(offset, half, gathered(offset, half, half, ()))
@@ -511,14 +533,9 @@
 
     @pl.when(core == 0)
     def _():
-        share(3)
         share(0)
 
-    for shift in (1, 3):
-        core_sum(shift, 0)
-        core_sum(shift, 1)
-    place_copy(1, 1).start()
-    place_copy(3, 0).start()
+    pl.when(core == 1)(next_places)
     att_ref[...] = dot(values, soft_r).T.astype(BF16)
     att_copy = pltpu.make_async_copy(att_ref, att_any, local.at[3])
     att_copy.start()
@@ -533,13 +550,14 @@
         for sign in (1, -1):
             total = gathered(6 * sign, half, -1, ((5 * sign, -1), (7 * sign, -1)))
             pass_on(6 * sign, half, total + eighth(sign) * part_of(zland, 8, half))
+        if half == 0:
+            merge(1, 0)
+            merge(3, 1)
     sums_landed(0, len(FAR))
     for which, sign in enumerate((1, -1)):
         total = spair[...] + eighth(sign) * sland[8]
         spart[which] = total + sland[(5 * sign) % NZ] + sland[(7 * sign) % NZ]
         back_sums(6 * sign, spart.at[which]).start()
-    merge(1, 0)
-    merge(3, 1)
     core_sum(0, 0)
     core_sum(0, 1)
     for sign in (1, -1):
@@ -634,7 +652,7 @@
         ),
         in_specs=[
             pl.BlockSpec(memory_space=pltpu.HBM),
-            pl.BlockSpec(memory_space=VMEM),
+            pl.BlockSpec(memory_space=pltpu.HBM),
             pl.BlockSpec(memory_space=pltpu.HBM),
             pl.BlockSpec(memory_space=pltpu.HBM),
         ],
@@ -649,6 +667,7 @@
             VMEM((FEAT, PATCHES), BF16),
             VMEM((ROWS, 3 * HDIM), F32),
             VMEM((D, 3 * HDIM), BF16),
+            VMEM((1, FEAT), BF16),
             VMEM((PATCHES, HDIM), BF16),
             VMEM((NMP, FEAT, PATCHES), BF16),
             VMEM((NMP, 1, 128), F32),
@@ -674,7 +693,7 @@
             VMEM((ROWS, 3 * HDIM), BF16),
             VMEM((1, 128), F32),
             VMEM((2 * CHIPS - 1, 1, 128), F32),
-            dma((6,)),
+            dma((7,)),
             dma((2,)),
             dma((2, len(GATHER_SLOTS))),
             dma((1,)),

time: 66.7 us -> 65.6 us (0.984)
  Pallas kernels: 65.9 us -> 64.8 us
    pallas_call x1, Pallas kernels: 64.1 us -> 63 us  [fused(): pl.pallas_call(fused_kernel, out_shape=(jax.ShapeDtypeStruct((PATCHES, HD...]
where the time goes in v7:
time: 65.6 us; the launch traced here: 65.4 us
  Pallas kernels  64.8 us (99%)
    pallas_call x1, Pallas kernels, fused(): pl.pallas_call(fused_kernel, out_shape=(jax.ShapeDtypeStruct((PATCHES, HD...  63 us
    pallas_call x1, Pallas kernels, finish(): pl.pallas_call(finish_kernel, out_shape=(jax.ShapeDtypeStruct((PATCHES, H...  1.77 us

profile of v7, /device:TPU:1, one launch (start us, length us, event | category | flops | bytes accessed | tf_op | source)
XLA Modules:
  0.0 65.4 jit_solution(11552181501726037015)
XLA Ops:
  0.6 63.0 %shard_map.75 = (bf16[256,128]{1,0:T(8,128)(2,1)}, bf16[96,256]{1,0:T(8,128)(2,1)}, f32[192,384]{1,0:T(8,128)}, f32[1,128]{1,0:T(1,128)}) custom-call(bf16[96,256]{1,0:T(8,128)(2,1)} %bitcast.6, bf16[1,96]{1,0:T(2,128)(2,1)} %bitcast.7, bf16[3072,384]{1,0:T(8,128)(2,1)} %bitcast.5, bf16[256,128]{1,0:T(8,128)(2,1)} %do_any.1), custom_call_target="tpu_custom_call" | custom-call | tf_op jit(solution)/shard_map/pallas_call | solution.py:645
  63.6 1.8 %shard_map.76 = (bf16[256,128]{1,0:T(8,128)(2,1)}, bf16[96,256]{1,0:T(8,128)(2,1)}, f32[192,1,384]{2,1,0:T(1,128)}, f32[1,96]{1,0:T(1,128)}) custom-call(bf16[256,128]{1,0:T(8,128)(2,1)} %get-tuple-element.12.att_in, bf16[96,256]{1,0:T(8,128)(2,1)} %get-tuple-element.13.ig_in, f32[192,384]{1,0:T(8,128)} %get-tuple-element.14.wg_in, ...), custom_call_target="tpu_custom_call" | custom-call | tf_op jit(solution)/shard_map/pallas_call | solution.py:746

commit v8 on v7

--- a/solution.py
+++ b/solution.py
@@ -115,6 +115,7 @@
     wt_ref,
     rows_ref,
     gb_ref,
+    gw_ref,
     nt_ref,
     hg_ref,
     hgt_ref,
@@ -473,6 +474,7 @@
     def _():
         for shift in shifts:
             share(shift)
+        gw_ref[...] = gain_product(theirs)
 
     pull_rows(theirs)
     for offset in FIVES:
@@ -490,8 +492,9 @@
     def _():
         share(2)
         share(1)
-
-    gain_weights = gain_weights + gain_product(theirs)
+        gw_ref[...] = gain_product(theirs)
+
+    gain_weights = gain_weights + gw_ref[...]
     hg_wide = hg.astype(F32)
     factor = jnp.concatenate([gain_weights, gain_weights], axis=1)
     sums[0] = jnp.sum(hg_wide * factor, axis=0, keepdims=True)
@@ -674,6 +677,7 @@
             VMEM((3 * HDIM, D), BF16),
             VMEM((NZ, 128), F32),
             VMEM((NMP, FEAT, 128), BF16),
+            VMEM((3 * HDIM, 128), F32),
             VMEM((NMP, FEAT, PATCHES), BF16),
             VMEM((3 * HDIM, PATCHES), BF16),
             VMEM((PATCHES, 3 * HDIM), BF16),

time: 65.6 us -> 66.5 us (1.014)
  Pallas kernels: 64.8 us -> 65.7 us
    pallas_call x1, Pallas kernels: 63 us -> 63.9 us  [fused(): pl.pallas_call(fused_kernel, out_shape=(jax.ShapeDtypeStruct((PATCHES, HD...]
where the time goes in v8:
time: 66.5 us; the launch traced here: 66.3 us
  Pallas kernels  65.7 us (99%)
    pallas_call x1, Pallas kernels, fused(): pl.pallas_call(fused_kernel, out_shape=(jax.ShapeDtypeStruct((PATCHES, HD...  63.9 us
    pallas_call x1, Pallas kernels, finish(): pl.pallas_call(finish_kernel, out_shape=(jax.ShapeDtypeStruct((PATCHES, H...  1.77 us

profile of v8, /device:TPU:1, one launch (start us, length us, event | category | flops | bytes accessed | tf_op | source)
XLA Modules:
  0.0 66.3 jit_solution(15696363786499176695)
XLA Ops:
  0.6 63.9 %shard_map.75 = (bf16[256,128]{1,0:T(8,128)(2,1)}, bf16[96,256]{1,0:T(8,128)(2,1)}, f32[192,384]{1,0:T(8,128)}, f32[1,128]{1,0:T(1,128)}) custom-call(bf16[96,256]{1,0:T(8,128)(2,1)} %bitcast.6, bf16[1,96]{1,0:T(2,128)(2,1)} %bitcast.7, bf16[3072,384]{1,0:T(8,128)(2,1)} %bitcast.5, bf16[256,128]{1,0:T(8,128)(2,1)} %do_any.1), custom_call_target="tpu_custom_call" | custom-call | tf_op jit(solution)/shard_map/pallas_call | solution.py:648
  64.6 1.8 %shard_map.76 = (bf16[256,128]{1,0:T(8,128)(2,1)}, bf16[96,256]{1,0:T(8,128)(2,1)}, f32[192,1,384]{2,1,0:T(1,128)}, f32[1,96]{1,0:T(1,128)}) custom-call(bf16[256,128]{1,0:T(8,128)(2,1)} %get-tuple-element.12.att_in, bf16[96,256]{1,0:T(8,128)(2,1)} %get-tuple-element.13.ig_in, f32[192,384]{1,0:T(8,128)} %get-tuple-element.14.wg_in, ...), custom_call_target="tpu_custom_call" | custom-call | tf_op jit(solution)/shard_map/pallas_call | solution.py:750

commit v9 on v7

--- a/solution.py
+++ b/solution.py
@@ -471,7 +471,7 @@
 
     @pl.when(core == 1)
     def _():
-        for shift in shifts:
+        for shift in shifts[:-1]:
             share(shift)
 
     pull_rows(theirs)
@@ -531,10 +531,7 @@
     for offset in NEAR:
         back(offset).start()
 
-    @pl.when(core == 0)
-    def _():
-        share(0)
-
+    share(0)
     pl.when(core == 1)(next_places)
     att_ref[...] = dot(values, soft_r).T.astype(BF16)
     att_copy = pltpu.make_async_copy(att_ref, att_any, local.at[3])

time: 65.6 us -> 65.6 us (level)
  no operation moved by 1% of the time
where the time goes in v9:
time: 65.6 us; the launch traced here: 65.5 us
  Pallas kernels  64.8 us (99%)
    pallas_call x1, Pallas kernels, fused(): pl.pallas_call(fused_kernel, out_shape=(jax.ShapeDtypeStruct((PATCHES, HD...  63 us
    pallas_call x1, Pallas kernels, finish(): pl.pallas_call(finish_kernel, out_shape=(jax.ShapeDtypeStruct((PATCHES, H...  1.77 us

profile of v9, /device:TPU:1, one launch (start us, length us, event | category | flops | bytes accessed | tf_op | source)
XLA Modules:
  0.0 65.5 jit_solution(5327966235884665128)
XLA Ops:
  0.6 63.0 %shard_map.75 = (bf16[256,128]{1,0:T(8,128)(2,1)}, bf16[96,256]{1,0:T(8,128)(2,1)}, f32[192,384]{1,0:T(8,128)}, f32[1,128]{1,0:T(1,128)}) custom-call(bf16[96,256]{1,0:T(8,128)(2,1)} %bitcast.6, bf16[1,96]{1,0:T(2,128)(2,1)} %bitcast.7, bf16[3072,384]{1,0:T(8,128)(2,1)} %bitcast.5, bf16[256,128]{1,0:T(8,128)(2,1)} %do_any.1), custom_call_target="tpu_custom_call" | custom-call | tf_op jit(solution)/shard_map/pallas_call | solution.py:642
  63.7 1.8 %shard_map.76 = (bf16[256,128]{1,0:T(8,128)(2,1)}, bf16[96,256]{1,0:T(8,128)(2,1)}, f32[192,1,384]{2,1,0:T(1,128)}, f32[1,96]{1,0:T(1,128)}) custom-call(bf16[256,128]{1,0:T(8,128)(2,1)} %get-tuple-element.12.att_in, bf16[96,256]{1,0:T(8,128)(2,1)} %get-tuple-element.13.ig_in, f32[192,384]{1,0:T(8,128)} %get-tuple-element.14.wg_in, ...), custom_call_target="tpu_custom_call" | custom-call | tf_op jit(solution)/shard_map/pallas_call | solution.py:743
